TPU v7x, 128 devices: a whole 4x4x4 slice. The times are simulated.
128 devices in a mesh: row: 16 (over z, y_lo, core), col: 8 (over x, y_hi).
Axes of the slice: x: 4, y: 4 (y_hi: 2, y_lo: 2; y = y_hi * 2 + y_lo), z: 4, core: 2. Of those that a mesh axis runs over, the one named last changes fastest.
Arguments:
- pair_in: bfloat16 [512, 512, 128], P('row', 'col'), may hold values from -6 to 6
- atoms_in: bfloat16 [12288, 128], P(('row', 'col')), may hold values from -6 to 6
- atom_token: int32 [12288], P(('row', 'col')), may hold values from 0 to 511, never falling along the last dimension, each value on 1 to 48 neighbouring positions
- atom_mask: int32 [12288], P(('row', 'col')), may hold values 0 or 1
- atom_weights: bfloat16 [5, 128, 128], replicated, may hold values from -0.5 to 0.5
- atom_trans_in: bfloat16 [2, 128, 256], replicated, may hold values from -0.5 to 0.5
- atom_trans_out: bfloat16 [256, 128], replicated, may hold values from -0.375 to 0.375
- token_in: bfloat16 [128, 384], replicated, may hold values from -0.5 to 0.5
- token_out: bfloat16 [384, 384], replicated, may hold values from -0.3125 to 0.3125
- tri_out_weights: bfloat16 [6, 128, 128], replicated, may hold values from -0.5 to 0.5
- tri_in_weights: bfloat16 [6, 128, 128], replicated, may hold values from -0.5 to 0.5
- pair_trans_in: bfloat16 [2, 128, 512], replicated, may hold values from -0.5 to 0.5
- pair_trans_out: bfloat16 [512, 128], replicated, may hold values from -0.25 to 0.25
Outputs:
- pair_out: bfloat16 [512, 512, 128], P('row', 'col')
- atoms_out: bfloat16 [12288, 128], P(('row', 'col'))
Inputs may be any that keep to these rules, and one draw needn't show every extreme that they name: `atom_token`: never falls from slot to slot; every token has 1 to 48 slots, and some token exactly 48.
All inputs are finite; a program needn't handle non-finite values. No bound on the sum of `atom_mask` on one device may be relied on, other than what follows from the above.
Results may differ from a plain program's by a relative error of at most 0.015.
Values may be sent and summed in bfloat16 or wider, within the bound.
A program may use at most 128 MiB of HBM per device.

v0:
```python
import jax
import jax.numpy as jnp
from jax import lax
from jax.sharding import PartitionSpec as P

HEADS = 4
QWIN = 32
KWIN = 128
SIDE = 48


epsilon = 1e-05


def with_halo(block, sides, width):
    for axis, dim in sides:
        count = lax.axis_size(axis)
        forward = [(i, i + 1) for i in range(count - 1)]
        backward = [(target, source) for source, target in forward]
        low = lax.ppermute(
            lax.slice_in_dim(block, block.shape[dim] - width, None, axis=dim), axis, forward
        )
        high = lax.ppermute(lax.slice_in_dim(block, 0, width, axis=dim), axis, backward)
        block = jnp.concatenate([low, block, high], axis=dim)
    return block


def layer_norm(values):
    values = values.astype(jnp.float32)
    center = values - jnp.mean(values, -1, keepdims=True)
    spread = jnp.mean(center * center, -1, keepdims=True)
    return center * lax.rsqrt(spread + epsilon)


def linear(inputs, weight):
    return jnp.einsum("...k,kn->...n", inputs, weight, preferred_element_type=jnp.float32)


def edge_terms(pair_state, weights):
    normed = layer_norm(pair_state).astype(jnp.bfloat16)
    left_edge = (jax.nn.sigmoid(linear(normed, weights[0])) * linear(normed, weights[1])).astype(
        jnp.bfloat16
    )
    right_edge = (jax.nn.sigmoid(linear(normed, weights[2])) * linear(normed, weights[3])).astype(
        jnp.bfloat16
    )
    tri_gate = jax.nn.sigmoid(linear(normed, weights[4]))
    return (left_edge, right_edge, tri_gate)


def finish(pair_state, product, tri_gate, weight):
    normed = layer_norm(product).astype(jnp.bfloat16)
    return pair_state + tri_gate * linear(normed, weight)


def project_keys(normed, atom_weights):
    return jnp.concatenate(
        [linear(normed, atom_weights[1]), linear(normed, atom_weights[2])], 1
    ).astype(jnp.bfloat16)


def attend(queries, wide_kv, wide_keep):
    slot_count, atom_width = queries.shape
    window_count = slot_count // QWIN
    head_dim = atom_width // HEADS
    starts = jnp.arange(window_count, dtype=jnp.int32) * QWIN - (KWIN - QWIN) // 2 + SIDE
    key_index = starts[:, None] + jnp.arange(KWIN, dtype=jnp.int32)[None, :]
    window_kv = jnp.take(wide_kv, key_index, axis=0)
    window_keep = jnp.take(wide_keep, key_index, axis=0)
    query_slot = jnp.arange(slot_count, dtype=jnp.int32).reshape(window_count, QWIN)
    allowed = (window_keep[:, None, :] > 0) | (
        (key_index - SIDE)[:, None, :] == query_slot[:, :, None]
    )
    window_query = queries.reshape(window_count, QWIN, HEADS, head_dim)
    window_keys = window_kv[..., :atom_width].reshape(window_count, KWIN, HEADS, head_dim)
    window_values = window_kv[..., atom_width:].reshape(window_count, KWIN, HEADS, head_dim)
    scores = jnp.einsum(
        "wqhd,wkhd->whqk", window_query, window_keys, preferred_element_type=jnp.float32
    ) * head_dim ** (-0.5)
    raw_weight = jnp.where(allowed[:, None, :, :], jnp.exp(scores), 0.0)
    attention_weights = (raw_weight / jnp.sum(raw_weight, -1, keepdims=True)).astype(jnp.bfloat16)
    attended = jnp.einsum(
        "whqk,wkhd->wqhd", attention_weights, window_values, preferred_element_type=jnp.float32
    )
    return attended.reshape(slot_count, atom_width)


def body(
    pair_in,
    atoms_in,
    atom_token,
    atom_mask,
    atom_weights,
    atom_trans_in,
    atom_trans_out,
    token_in,
    token_out,
    tri_out_weights,
    tri_in_weights,
    pair_trans_in,
    pair_trans_out,
):
    atom_normed = layer_norm(atoms_in).astype(jnp.bfloat16)
    queries = linear(atom_normed, atom_weights[0]).astype(jnp.bfloat16)
    atom_gate = jax.nn.sigmoid(linear(atom_normed, atom_weights[3]))
    keep_flags = atom_mask.astype(jnp.bfloat16)
    key_values = project_keys(atom_normed, atom_weights)
    wide_kv, wide_keep = (
        with_halo(key_values, ((("row", "col"), 0),), SIDE),
        with_halo(keep_flags, ((("row", "col"), 0),), SIDE),
    )
    attended = attend(queries, wide_kv, wide_keep)
    gated = (atom_gate * attended).astype(jnp.bfloat16)
    atom_resid = atoms_in.astype(jnp.float32) + linear(gated, atom_weights[4])
    resid_normed = layer_norm(atom_resid).astype(jnp.bfloat16)
    atom_hidden = (
        jax.nn.silu(linear(resid_normed, atom_trans_in[0])) * linear(resid_normed, atom_trans_in[1])
    ).astype(jnp.bfloat16)
    atom_mid = atom_resid + linear(atom_hidden, atom_trans_out)
    atom_feature = jax.nn.relu(linear(atom_mid.astype(jnp.bfloat16), token_in)).astype(jnp.bfloat16)
    row_tokens, col_tokens, pair_width = pair_in.shape
    token_total = row_tokens * lax.axis_size("row")
    member = (atom_token[None, :] == jnp.arange(token_total, dtype=jnp.int32)[:, None]) & (
        atom_mask[None, :] == 1
    )
    partial_sums = jnp.dot(
        member.astype(jnp.bfloat16), atom_feature, preferred_element_type=jnp.float32
    )
    partial_counts = jnp.sum(member.astype(jnp.float32), 1)
    token_sums, token_counts = lax.psum((partial_sums, partial_counts), ("row", "col"))
    single = (token_sums / jnp.maximum(token_counts, 1.0)[:, None]).astype(jnp.bfloat16)
    token_proj = jnp.dot(single, token_out, preferred_element_type=jnp.float32)
    atoms_out = (atom_mid + jnp.take(token_proj[:, 2 * pair_width :], atom_token, axis=0)).astype(
        jnp.bfloat16
    )
    row_index = lax.axis_index("row")
    col_index = lax.axis_index("col")
    left_add = lax.dynamic_slice_in_dim(
        token_proj[:, :pair_width], row_index * row_tokens, row_tokens, 0
    )
    right_add = lax.dynamic_slice_in_dim(
        token_proj[:, pair_width : 2 * pair_width], col_index * col_tokens, col_tokens, 0
    )
    pair_state = pair_in.astype(jnp.float32) + left_add[:, None, :] + right_add[None, :, :]
    left_edge, right_edge, tri_gate = edge_terms(pair_state, tri_out_weights)
    out_terms = jnp.einsum(
        "ikc,jkc->ijc",
        left_edge,
        lax.all_gather(right_edge, "row", axis=0, tiled=True),
        preferred_element_type=jnp.float32,
    )
    product = lax.psum_scatter(
        out_terms.astype(jnp.bfloat16), "col", scatter_dimension=1, tiled=True
    ).astype(jnp.float32)
    pair_state = finish(pair_state, product, tri_gate, tri_out_weights[5])
    left_edge, right_edge, tri_gate = edge_terms(pair_state, tri_in_weights)
    left_rows = lax.all_gather(left_edge, "col", axis=1, tiled=True)
    product = lax.psum_scatter(
        jnp.einsum(
            "kic,kjc->ijc", left_rows, right_edge, preferred_element_type=jnp.float32
        ).astype(jnp.bfloat16),
        "row",
        scatter_dimension=0,
        tiled=True,
    ).astype(jnp.float32)
    pair_state = finish(pair_state, product, tri_gate, tri_in_weights[5])
    pair_normed = layer_norm(pair_state).astype(jnp.bfloat16)
    pair_hidden = (
        jax.nn.silu(linear(pair_normed, pair_trans_in[0])) * linear(pair_normed, pair_trans_in[1])
    ).astype(jnp.bfloat16)
    pair_out = (pair_state + linear(pair_hidden, pair_trans_out)).astype(jnp.bfloat16)
    return (pair_out, atoms_out)


def solution(mesh):
    placed = (
        P("row", "col", None),
        P(("row", "col"), None),
        P(("row", "col")),
        P(("row", "col")),
        P(),
        P(),
        P(),
        P(),
        P(),
        P(),
        P(),
        P(),
        P(),
    )
    return jax.shard_map(
        body,
        mesh=mesh,
        in_specs=placed,
        out_specs=(P("row", "col", None), P(("row", "col"), None)),
        check_vma=False,
    )
```

profile of v0, /device:TPU:1, one launch (start us, length us, event | category | flops | bytes accessed | tf_op | source)
XLA Modules:
  0.0 601.0 jit_solution(8747528252179857276)
XLA Ops:
  11.2 8.4 %collective-permute-start.1 = (bf16[48,256]{1,0:T(8,128)(2,1)S(1)}, bf16[48,256]{1,0:T(8,128)(2,1)S(1)}, u32[]{:S(2)}, u32[]{:S(2)}) collective-permute-start(bf16[48,256]{1,0:T(8,128)(2,1)S(1)} %get-tuple-element.8), channel_id=1, source_target_pairs={{1,0},{2,1},{3,2},{4,3},{5,4},{6,5},{7,6},{8,7},{9,8},{10,9},{11,1... | collective-permute-start | bytes 73736 | tf_op jit(solution)/shard_map/ppermute | solution.py:23
  19.6 1.9 collective-permute-start
  22.3 7.2 %collective-permute-start.3 = (bf16[48]{0:T(256)(128)(2,1)S(1)}, bf16[48]{0:T(256)(128)(2,1)S(1)}, u32[]{:S(2)}, u32[]{:S(2)}) collective-permute-start(bf16[48]{0:T(256)(128)(2,1)S(1)} %get-tuple-element.12), channel_id=1, source_target_pairs={{1,0},{2,1},{3,2},{4,3},{5,4},{6,5},{7,6},{8,7},{9,8},{10,9},{11,1... | collective-permute-start | bytes 296 | tf_op jit(solution)/shard_map/ppermute | solution.py:23
  29.5 1.9 collective-permute-start.2
  33.4 4.6 collective-permute-done.2
  38.1 2.7 gather_fusion.1
  41.0 2.1 gather_fusion
  47.5 66.1 %psum.15 = f32[512]{0:T(512)S(1)} all-reduce(f32[512]{0:T(512)S(1)} %convert_reduce_fusion.2), channel_id=1, replica_groups=mesh['row'=16,'col'=8] {'row','col'}, use_global_device_ids=true, to_apply=%region_7.8 | all-reduce | flops 512 | bytes 4096 | tf_op jit(solution)/shard_map/psum | solution.py:130
  113.7 78.1 %all-reduce.2.cloned.1.call-done = f32[512,384]{1,0:T(8,128)} async-done(((f32[512,384]{1,0:T(8,128)}), f32[512,384]{1,0:T(8,128)}) %all-reduce.2.cloned.1.call-update) | async-done | bytes 786448 | tf_op jit(solution)/shard_map/psum | solution.py:130
  200.5 47.4 %all-gather.3.cloned.1.call-done = bf16[512,64,128]{2,1,0:T(8,128)(2,1)} async-done(((bf16[32,64,128]{2,1,0:T(8,128)(2,1)}), bf16[512,64,128]{2,1,0:T(8,128)(2,1)}) %all-gather.3.cloned.1.call-update) | async-done | bytes 8388624 | tf_op jit(solution)/shard_map/all_gather | solution.py:149
  248.0 23.7 %copy.93 = bf16[512,64,128]{1,0,2:T(8,128)(2,1)} copy(bf16[512,64,128]{2,1,0:T(8,128)(2,1)} %all-gather.3.cloned.1.call-done) | data formatting | bytes 16777216 | tf_op jit(solution)/shard_map/all_gather | solution.py:149
  271.7 10.7 %convert_bitcast_fusion.1 = bf16[32,512,128]{1,0,2:T(8,128)(2,1)} fusion(bf16[512,64,128]{1,0,2:T(8,128)(2,1)} %copy.93, bf16[32,64,128]{1,0,2:T(8,128)(2,1)S(1)} %copy.94), kind=kOutput, calls=%fused_computation.5 | convolution fusion | flops 270532608 | bytes 13107200 | tf_op jit(solution)/shard_map/ikc,jkc->ijc/dot_general | solution.py:146
  282.4 9.1 %copy.95 = bf16[32,512,128]{2,0,1:T(8,128)(2,1)} copy(bf16[32,512,128]{1,0,2:T(8,128)(2,1)} %convert_bitcast_fusion.1) | data formatting | bytes 8388608 | tf_op jit(solution)/shard_map/convert_element_type | solution.py:153
  291.6 84.3 %reduce-scatter.3.cloned.1.call-done = bf16[32,64,128]{2,0,1:T(8,128)(2,1)} async-done(((bf16[32,512,128]{2,0,1:T(8,128)(2,1)}), bf16[32,64,128]{2,0,1:T(8,128)(2,1)}) %reduce-scatter.3.cloned.1.call-update) | async-done | bytes 524304 | tf_op jit(solution)/shard_map/reduce_scatter | solution.py:152
  377.5 1.7 fusion.51
  388.4 67.8 %all-gather.5.cloned.1.call-done = bf16[32,512,128]{2,1,0:T(8,128)(2,1)} async-done(((bf16[32,64,128]{2,1,0:T(8,128)(2,1)}), bf16[32,512,128]{2,1,0:T(8,128)(2,1)}) %all-gather.5.cloned.1.call-update) | async-done | bytes 4194320 | tf_op jit(solution)/shard_map/all_gather | solution.py:157
  456.2 7.9 %copy.102 = bf16[32,512,128]{1,0,2:T(8,128)(2,1)} copy(bf16[32,512,128]{2,1,0:T(8,128)(2,1)} %all-gather.5.cloned.1.call-done) | data formatting | bytes 8388608 | tf_op jit(solution)/shard_map/all_gather | solution.py:157
  464.1 7.8 %convert_bitcast_fusion = bf16[512,64,128]{0,1,2:T(8,128)(2,1)} fusion(bf16[32,64,128]{1,0,2:T(8,128)(2,1)S(1)} %copy.101, bf16[32,512,128]{1,0,2:T(8,128)(2,1)} %copy.102), kind=kOutput, calls=%fused_computation.3 | convolution fusion | flops 272629760 | bytes 13107200 | tf_op jit(solution)/shard_map/kic,kjc->ijc/dot_general | solution.py:159
  471.9 13.7 %copy.103 = bf16[512,64,128]{2,1,0:T(8,128)(2,1)} copy(bf16[512,64,128]{0,1,2:T(8,128)(2,1)} %convert_bitcast_fusion) | data formatting | bytes 16777216 | tf_op jit(solution)/shard_map/convert_element_type | solution.py:161
  486.9 93.2 %reduce-scatter.5.cloned.1.call-done = bf16[32,64,128]{2,1,0:T(8,128)(2,1)} async-done(((bf16[512,64,128]{2,1,0:T(8,128)(2,1)}), bf16[32,64,128]{2,1,0:T(8,128)(2,1)}) %reduce-scatter.5.cloned.1.call-update) | async-done | bytes 524304 | tf_op jit(solution)/shard_map/reduce_scatter | solution.py:158
  581.6 1.7 fusion.49
  583.3 1.8 fusion.56
  587.1 2.5 fusion.55
  589.6 4.9 fusion.28
  (118 shorter events, 35.3 us)
Async XLA Ops:
  7.2 184.6 %copy-start = (bf16[384,384]{1,0:T(8,128)(2,1)S(1)}, bf16[384,384]{1,0:T(8,128)(2,1)}, u32[]{:S(2)}) copy-start(bf16[384,384]{1,0:T(8,128)(2,1)} %param.21) | copy-start | bytes 884740
  7.2 36.8 %copy-start.3 = (bf16[96,128]{1,0:T(8,128)(2,1)S(1)}, bf16[96,128]{1,0:T(8,128)(2,1)}, u32[]{:S(2)}) copy-start(bf16[96,128]{1,0:T(8,128)(2,1)} %param.14) | copy-start | bytes 73732
  7.2 38.2 %copy-start.8 = (bf16[2,128,256]{2,1,0:T(8,128)(2,1)S(1)}, bf16[2,128,256]{2,1,0:T(8,128)(2,1)}, u32[]{:S(2)}) copy-start(bf16[2,128,256]{2,1,0:T(8,128)(2,1)} %param.18) | copy-start | bytes 393220
  7.2 38.4 %copy-start.11 = (bf16[256,128]{1,0:T(8,128)(2,1)S(1)}, bf16[256,128]{1,0:T(8,128)(2,1)}, u32[]{:S(2)}) copy-start(bf16[256,128]{1,0:T(8,128)(2,1)} %param.19) | copy-start | bytes 196612
  7.2 38.8 %copy-start.4 = (bf16[128,384]{1,0:T(8,128)(2,1)S(1)}, bf16[128,384]{1,0:T(8,128)(2,1)}, u32[]{:S(2)}) copy-start(bf16[128,384]{1,0:T(8,128)(2,1)} %param.20) | copy-start | bytes 294916
  7.2 38.8 %copy-start.9 = (s32[96]{0:T(128)S(1)}, s32[96]{0:T(128)}, u32[]{:S(2)}) copy-start(s32[96]{0:T(128)} %param.15) | copy-start | bytes 1156
  7.2 184.5 %all-reduce.2.cloned.1.call-start = ((), (), s32[]{:S(2)}) async-start(), calls=%async_computation.2 | async-start | bytes 1572864 | tf_op jit(solution)/shard_map/psum | solution.py:130
  11.2 29.8 %collective-permute-start.1 = (bf16[48,256]{1,0:T(8,128)(2,1)S(1)}, bf16[48,256]{1,0:T(8,128)(2,1)S(1)}, u32[]{:S(2)}, u32[]{:S(2)}) collective-permute-start(bf16[48,256]{1,0:T(8,128)(2,1)S(1)} %get-tuple-element.8), channel_id=1, source_target_pairs={{1,0},{2,1},{3,2},{4,3},{5,4},{6,5},{7,6},{8,7},{9,8},{10,9},{11,1... | collective-permute-start | bytes 73736 | tf_op jit(solution)/shard_map/ppermute | solution.py:23
  19.6 21.4 %collective-permute-start = (bf16[48,256]{1,0:T(8,128)(2,1)S(1)}, bf16[48,256]{1,0:T(8,128)(2,1)S(1)}, u32[]{:S(2)}, u32[]{:S(2)}) collective-permute-start(bf16[48,256]{1,0:T(8,128)(2,1)S(1)} %get-tuple-element.7), channel_id=1, source_target_pairs={{0,1},{1,2},{2,3},{3,4},{4,5},{5,6},{6,7},{7,8},{8,9},{9,10},{10,1... | collective-permute-start | bytes 73736 | tf_op jit(solution)/shard_map/ppermute | solution.py:20
  22.3 11.1 %collective-permute-start.3 = (bf16[48]{0:T(256)(128)(2,1)S(1)}, bf16[48]{0:T(256)(128)(2,1)S(1)}, u32[]{:S(2)}, u32[]{:S(2)}) collective-permute-start(bf16[48]{0:T(256)(128)(2,1)S(1)} %get-tuple-element.12), channel_id=1, source_target_pairs={{1,0},{2,1},{3,2},{4,3},{5,4},{6,5},{7,6},{8,7},{9,8},{10,9},{11,1... | collective-permute-start | bytes 296 | tf_op jit(solution)/shard_map/ppermute | solution.py:23
  29.5 8.5 %collective-permute-start.2 = (bf16[48]{0:T(256)(128)(2,1)S(1)}, bf16[48]{0:T(256)(128)(2,1)S(1)}, u32[]{:S(2)}, u32[]{:S(2)}) collective-permute-start(bf16[48]{0:T(256)(128)(2,1)S(1)} %get-tuple-element.11), channel_id=1, source_target_pairs={{0,1},{1,2},{2,3},{3,4},{4,5},{5,6},{6,7},{7,8},{8,9},{9,10},{10,1... | collective-permute-start | bytes 296 | tf_op jit(solution)/shard_map/ppermute | solution.py:20
  43.7 149.8 %copy-start.2 = (bf16[32,64,128]{2,1,0:T(8,128)(2,1)S(1)}, bf16[32,64,128]{2,1,0:T(8,128)(2,1)}, u32[]{:S(2)}) copy-start(bf16[32,64,128]{2,1,0:T(8,128)(2,1)} %param.13) | copy-start | bytes 1572868
  45.6 148.9 %copy-start.6 = (bf16[6,128,128]{2,1,0:T(8,128)(2,1)S(1)}, bf16[6,128,128]{2,1,0:T(8,128)(2,1)}, u32[]{:S(2)}) copy-start(bf16[6,128,128]{2,1,0:T(8,128)(2,1)} %param.22) | copy-start | bytes 589828
  47.4 200.6 %all-gather.3.cloned.1.call-start = ((), (), s32[]{:S(2)}) async-start(), calls=%async_computation.3 | async-start | bytes 8912896 | tf_op jit(solution)/shard_map/all_gather | solution.py:149
  197.0 178.9 %reduce-scatter.3.cloned.1.call-start = ((), (), s32[]{:S(2)}) async-start(), calls=%async_computation.4 | async-start | bytes 4718592 | tf_op jit(solution)/shard_map/reduce_scatter | solution.py:152
  291.5 164.7 %all-gather.5.cloned.1.call-start = ((), (), s32[]{:S(2)}) async-start(), calls=%async_computation.5 | async-start | bytes 4718592 | tf_op jit(solution)/shard_map/all_gather | solution.py:157
  381.3 2.2 copy-start.7
  385.1 195.1 %reduce-scatter.5.cloned.1.call-start = ((), (), s32[]{:S(2)}) async-start(), calls=%async_computation.6 | async-start | bytes 8912896 | tf_op jit(solution)/shard_map/reduce_scatter | solution.py:158
  583.3 3.8 copy-start.5
  586.4 3.2 copy-start.10
  589.6 4.9 copy-start.1
Sparse Core Ops, SparseCore 0:
  47.5 144.2 all-reduce.1
  197.1 50.8 all-gather.2
  291.7 84.2 reduce-scatter.2
  385.2 70.9 all-gather.4
  485.7 94.4 reduce-scatter.4
where the time goes:
time: 604 us; the launch traced here: 601 us
  waiting for transfers between devices  376 us (62%)
  blocking collectives  66.1 us (11%)
  local copies, waits for them, and re-layouts  64.1 us (11%)
  matrix products  45.3 us (8%)
  starting transfers between devices  20.1 us (3%)
  other arithmetic  15.4 us (3%)
  between operations  14.4 us (2%)
    reduce_scatter x1, waiting for transfers between devices, body(): lax.psum_scatter(jnp.einsum('kic,kjc->ijc', left_rows, right_edge, prefer...  93.2 us
    reduce_scatter x1, waiting for transfers between devices, body(): lax.psum_scatter(out_terms.astype(jnp.bfloat16), 'col', scatter_dimension...  84.3 us
    psum x1, waiting for transfers between devices, body(): lax.psum((partial_sums, partial_counts), ('row', 'col'))  78.1 us
    all_gather x1, waiting for transfers between devices, body(): left_rows = lax.all_gather(left_edge, 'col', axis=1, tiled=True)  67.8 us
    psum x1, blocking collectives, body(): lax.psum((partial_sums, partial_counts), ('row', 'col'))  66.1 us
    all_gather x1, waiting for transfers between devices, body(): lax.all_gather(right_edge, 'row', axis=0, tiled=True)  47.4 us
    all_gather x1, local copies, waits for them, and re-layouts, body(): lax.all_gather(right_edge, 'row', axis=0, tiled=True)  23.7 us
    dot_general x20, matrix products, linear(): jnp.einsum('...k,kn->...n', inputs, weight, preferred_element_type=jnp.fl...  23.4 us
  transfers between devices with their start and end apart: 9, of which 6 were waited for; matrix products, arithmetic and copies ran while one was open for 2% of the time, Pallas kernels for 0%

commit v1 on v0

--- a/solution.py
+++ b/solution.py
@@ -1,6 +1,8 @@
 import jax
 import jax.numpy as jnp
 from jax import lax
+from jax.experimental import pallas as pl
+from jax.experimental.pallas import tpu as pltpu
 from jax.sharding import PartitionSpec as P
 
 HEADS = 4
@@ -36,21 +38,231 @@
     return jnp.einsum("...k,kn->...n", inputs, weight, preferred_element_type=jnp.float32)
 
 
-def edge_terms(pair_state, weights):
-    normed = layer_norm(pair_state).astype(jnp.bfloat16)
-    left_edge = (jax.nn.sigmoid(linear(normed, weights[0])) * linear(normed, weights[1])).astype(
-        jnp.bfloat16
-    )
-    right_edge = (jax.nn.sigmoid(linear(normed, weights[2])) * linear(normed, weights[3])).astype(
-        jnp.bfloat16
-    )
-    tri_gate = jax.nn.sigmoid(linear(normed, weights[4]))
-    return (left_edge, right_edge, tri_gate)
-
-
-def finish(pair_state, product, tri_gate, weight):
-    normed = layer_norm(product).astype(jnp.bfloat16)
-    return pair_state + tri_gate * linear(normed, weight)
+def _peers(r, c, fn):
+    for m in range(1, 128):
+        n = (m * 45) % 128
+        fn(lax.rem(r + n // 8, 16), lax.rem(c + n % 8, 8))
+
+
+def _sigmoid(x):
+    return 0.5 * jnp.tanh(0.5 * x) + 0.5
+
+
+def _norm(x):
+    center = x - jnp.mean(x, 0, keepdims=True)
+    spread = jnp.mean(center * center, 0, keepdims=True)
+    return center * lax.rsqrt(spread + epsilon)
+
+
+def _dot(a, b):
+    return jnp.dot(a, b, preferred_element_type=jnp.float32)
+
+
+def _flip(x):
+    return jnp.transpose(x.astype(jnp.float32)).astype(jnp.bfloat16)
+
+
+def _pair_kernel(
+    pair_ref, left_ref, right_ref, out_w_ref, in_w_ref, tin_ref, tout_ref, result_ref,
+    state, normed, gate, rows32, weights, tin_t, tout_t,
+    send_l, send_r, send_p, recv_l, recv_r, recv_p, mat_l, mat_r, mat_p, wide,
+    sent, got, entered,
+):
+    r = lax.axis_index("row")
+    c = lax.axis_index("col")
+    me = r * 8 + c
+    barrier = pltpu.get_barrier_semaphore()
+
+    def greet(semaphore, row, col):
+        pl.semaphore_signal(
+            semaphore, inc=1, device_id=(row, col), device_id_type=pl.DeviceIdType.MESH
+        )
+
+    for step in range(1, 8):
+        greet(barrier, r, lax.rem(c + step, 8))
+    for step in range(1, 16):
+        greet(barrier, lax.rem(r + step, 16), c)
+
+    for w in range(6):
+        weights[pl.ds(w * 128, 128), :] = _flip(out_w_ref[w])
+        weights[pl.ds((6 + w) * 128, 128), :] = _flip(in_w_ref[w])
+    for w in range(2):
+        tin_t[pl.ds(w * 512, 512), :] = _flip(tin_ref[w])
+    tout_t[...] = _flip(tout_ref[...])
+
+    def start_state(a, _):
+        natural = jnp.concatenate([pair_ref[a], pair_ref[a + 16]], 0).astype(jnp.float32)
+        right = right_ref[...]
+        natural = natural + jnp.concatenate(
+            [right + left_ref[pl.ds(a, 1), :], right + left_ref[pl.ds(a + 16, 1), :]], 0
+        )
+        turned = jnp.transpose(natural)
+        state[a] = turned
+        normed[a] = _norm(turned).astype(jnp.bfloat16)
+        return 0
+
+    lax.fori_loop(0, 16, start_state, 0)
+
+    pl.semaphore_wait(barrier, 22)
+    for step in range(1, 16):
+        greet(entered, lax.rem(r + step, 16), c)
+    pl.semaphore_wait(entered, 15)
+
+    def pack(target):
+        def move(d, _):
+            target[pl.ds(d * 8, 8)] = (
+                rows32[pl.ds(d * 128, 128), :].reshape(8, 16, 128).astype(jnp.bfloat16)
+            )
+            return 0
+
+        lax.fori_loop(0, 16, move, 0)
+
+    def launch(source, target, k):
+        target[me] = source[me]
+
+        def one(row, col):
+            pltpu.make_async_remote_copy(
+                src_ref=source.at[row * 8 + col],
+                dst_ref=target.at[me],
+                send_sem=sent.at[k],
+                recv_sem=got.at[k],
+                device_id=(row, col),
+                device_id_type=pl.DeviceIdType.MESH,
+            ).start()
+
+        _peers(r, c, one)
+
+    def finish_copies(source, target, k):
+        part = pl.ds(0, 127)
+        pltpu.make_async_copy(source.at[part], source.at[part], sent.at[k]).wait()
+        pltpu.make_async_copy(target.at[part], target.at[part], got.at[k]).wait()
+
+    def edges(base, first):
+        def chunk(a, _):
+            both = _dot(weights[pl.ds((base + first) * 128, 256), :], normed[a])
+            rows32[pl.ds(a, 128, stride=16), :] = _sigmoid(both[:128]) * both[128:]
+            return 0
+
+        lax.fori_loop(0, 16, chunk, 0)
+
+    def gates(base):
+        def chunk(a, _):
+            gate[a] = _sigmoid(_dot(weights[pl.ds((base + 4) * 128, 128), :], normed[a]))
+            return 0
+
+        lax.fori_loop(0, 16, chunk, 0)
+
+    def assemble(source, target):
+        def block(row, _):
+            for q in range(4):
+                even = source[row * 8 + 2 * q]
+                odd = source[row * 8 + 2 * q + 1]
+                target[pl.ds(row * 32, 16), pl.ds(q * 128, 128)] = jnp.concatenate(
+                    [even[:, :64], odd[:, :64]], 1
+                )
+                target[pl.ds(row * 32 + 16, 16), pl.ds(q * 128, 128)] = jnp.concatenate(
+                    [even[:, 64:], odd[:, 64:]], 1
+                )
+            return 0
+
+        lax.fori_loop(0, 16, block, 0)
+
+    def split(source, target):
+        def block(row, _):
+            for q in range(4):
+                top = source[pl.ds(row * 32, 16), pl.ds(q * 128, 128)]
+                low = source[pl.ds(row * 32 + 16, 16), pl.ds(q * 128, 128)]
+                target[row * 8 + 2 * q] = jnp.concatenate([top[:, :64], low[:, :64]], 1)
+                target[row * 8 + 2 * q + 1] = jnp.concatenate([top[:, 64:], low[:, 64:]], 1)
+            return 0
+
+        lax.fori_loop(0, 16, block, 0)
+
+    def triangle(t, after):
+        base = 6 * t
+        edges(base, 0)
+        pack(send_l.at[t])
+        launch(send_l.at[t], recv_l.at[t], 3 * t)
+        edges(base, 2)
+        pack(send_r.at[t])
+        launch(send_r.at[t], recv_r.at[t], 3 * t + 1)
+        gates(base)
+        finish_copies(send_l.at[t], recv_l.at[t], 3 * t)
+        assemble(recv_l.at[t], mat_l)
+        finish_copies(send_r.at[t], recv_r.at[t], 3 * t + 1)
+        assemble(recv_r.at[t], mat_r)
+        axis = 1 - t
+        mat_p[...] = lax.dot_general(
+            mat_l[...],
+            mat_r[...],
+            (((axis,), (axis,)), ((), ())),
+            preferred_element_type=jnp.float32,
+        ).astype(jnp.bfloat16)
+        split(mat_p, send_p.at[t])
+        launch(send_p.at[t], recv_p.at[t], 3 * t + 2)
+        finish_copies(send_p.at[t], recv_p.at[t], 3 * t + 2)
+
+        def widen(d, _):
+            rows32[pl.ds(d * 128, 128), :] = (
+                recv_p[t, pl.ds(d * 8, 8)].astype(jnp.float32).reshape(128, 128)
+            )
+            return 0
+
+        lax.fori_loop(0, 16, widen, 0)
+
+        def close(a, _):
+            product = _norm(rows32[pl.ds(a, 128, stride=16), :]).astype(jnp.bfloat16)
+            updated = state[a] + gate[a] * _dot(weights[pl.ds((base + 5) * 128, 128), :], product)
+            state[a] = updated
+            normed[a] = _norm(updated).astype(jnp.bfloat16)
+            if after is not None:
+                after(a, updated)
+            return 0
+
+        lax.fori_loop(0, 16, close, 0)
+
+    def transition(a, updated):
+        inner = _dot(tin_t[...], normed[a])
+        up = inner[:512]
+        hidden = (up * _sigmoid(up) * inner[512:]).astype(jnp.bfloat16)
+        final = jnp.transpose(updated + _dot(tout_t[...], hidden)).astype(jnp.bfloat16)
+        result_ref[a] = final[:64]
+        result_ref[a + 16] = final[64:]
+
+    triangle(0, None)
+    triangle(1, transition)
+
+
+def _pair_trunk(pair_in, left_add, right_add, out_w, in_w, tin, tout):
+    vmem = pl.BlockSpec(memory_space=pltpu.VMEM)
+    message = (2, 128, 16, 128)
+    return pl.pallas_call(
+        _pair_kernel,
+        out_shape=jax.ShapeDtypeStruct(pair_in.shape, jnp.bfloat16),
+        in_specs=[vmem] * 7,
+        out_specs=vmem,
+        scratch_shapes=[
+            pltpu.VMEM((16, 128, 128), jnp.float32),
+            pltpu.VMEM((16, 128, 128), jnp.bfloat16),
+            pltpu.VMEM((16, 128, 128), jnp.float32),
+            pltpu.VMEM((2048, 128), jnp.float32),
+            pltpu.VMEM((1536, 128), jnp.bfloat16),
+            pltpu.VMEM((1024, 128), jnp.bfloat16),
+            pltpu.VMEM((128, 512), jnp.bfloat16),
+        ]
+        + [pltpu.VMEM(message, jnp.bfloat16)] * 6
+        + [pltpu.VMEM((512, 512), jnp.bfloat16)] * 3
+        + [
+            pltpu.VMEM((8, 128), jnp.float32),
+            pltpu.SemaphoreType.DMA((6,)),
+            pltpu.SemaphoreType.DMA((6,)),
+            pltpu.SemaphoreType.REGULAR,
+        ],
+        compiler_params=pltpu.CompilerParams(
+            collective_id=0, has_side_effects=True, vmem_limit_bytes=48 * 1024 * 1024
+        ),
+        name="pair_trunk",
+    )(pair_in, left_add, right_add, out_w, in_w, tin, tout)
 
 
 def project_keys(normed, atom_weights):
@@ -141,34 +353,15 @@
     right_add = lax.dynamic_slice_in_dim(
         token_proj[:, pair_width : 2 * pair_width], col_index * col_tokens, col_tokens, 0
     )
-    pair_state = pair_in.astype(jnp.float32) + left_add[:, None, :] + right_add[None, :, :]
-    left_edge, right_edge, tri_gate = edge_terms(pair_state, tri_out_weights)
-    out_terms = jnp.einsum(
-        "ikc,jkc->ijc",
-        left_edge,
-        lax.all_gather(right_edge, "row", axis=0, tiled=True),
-        preferred_element_type=jnp.float32,
-    )
-    product = lax.psum_scatter(
-        out_terms.astype(jnp.bfloat16), "col", scatter_dimension=1, tiled=True
-    ).astype(jnp.float32)
-    pair_state = finish(pair_state, product, tri_gate, tri_out_weights[5])
-    left_edge, right_edge, tri_gate = edge_terms(pair_state, tri_in_weights)
-    left_rows = lax.all_gather(left_edge, "col", axis=1, tiled=True)
-    product = lax.psum_scatter(
-        jnp.einsum(
-            "kic,kjc->ijc", left_rows, right_edge, preferred_element_type=jnp.float32
-        ).astype(jnp.bfloat16),
-        "row",
-        scatter_dimension=0,
-        tiled=True,
-    ).astype(jnp.float32)
-    pair_state = finish(pair_state, product, tri_gate, tri_in_weights[5])
-    pair_normed = layer_norm(pair_state).astype(jnp.bfloat16)
-    pair_hidden = (
-        jax.nn.silu(linear(pair_normed, pair_trans_in[0])) * linear(pair_normed, pair_trans_in[1])
-    ).astype(jnp.bfloat16)
-    pair_out = (pair_state + linear(pair_hidden, pair_trans_out)).astype(jnp.bfloat16)
+    pair_out = _pair_trunk(
+        pair_in,
+        left_add,
+        right_add,
+        tri_out_weights,
+        tri_in_weights,
+        pair_trans_in,
+        pair_trans_out,
+    )
     return (pair_out, atoms_out)
 
 

time: 604 us -> 349 us (0.58)
  waiting for transfers between devices: 376 us -> 143 us
  Pallas kernels: 0 us -> 86.6 us
  local copies, waits for them, and re-layouts: 64.1 us -> 10 us
  matrix products: 45.3 us -> 6.48 us
  other arithmetic: 15.4 us -> 2.53 us
    reduce_scatter x2 -> x0, waiting for transfers between devices: 178 us -> none  [the longest x1 93.2 us: body(): lax.psum_scatter(jnp.einsum('kic,kjc->ijc', left_rows, right_edge, prefer...]
    all_gather x2 -> x0, waiting for transfers between devices: 115 us -> none  [the longest x1 67.8 us: body(): left_rows = lax.all_gather(left_edge, 'col', axis=1, tiled=True)]
    pallas_call x0 -> x1, Pallas kernels: none -> 86.6 us  [_pair_trunk(): pl.pallas_call(_pair_kernel, out_shape=jax.ShapeDtypeStruct(pair_in.shape...]
    psum x1, waiting for transfers between devices: 78.1 us -> 143 us  [body(): lax.psum((partial_sums, partial_counts), ('row', 'col'))]
    all_gather x2 -> x0, local copies, waits for them, and re-layouts: 31.6 us -> none  [the longest x1 23.7 us: body(): lax.all_gather(right_edge, 'row', axis=0, tiled=True)]
    convert_element_type x4 -> x0, local copies, waits for them, and re-layouts: 26 us -> none  [the longest x1 13.7 us: body(): product = lax.psum_scatter(jnp.einsum('kic,kjc->ijc', left_rows, right_ed...]
    dot_general x20 -> x6, matrix products: 23.4 us -> 3.15 us  [linear(): jnp.einsum('...k,kn->...n', inputs, weight, preferred_element_type=jnp.fl...]
    dot_general x2 -> x0, matrix products: 18.5 us -> none  [the longest x1 10.7 us: body(): jnp.einsum('ikc,jkc->ijc', left_edge, lax.all_gather(right_edge, 'row', a...]
  transfers between devices with their start and end apart: 9 -> 5, of which waited for: 6 -> 1; matrix products, arithmetic and copies ran while one was open for 2% -> 1% of each run, Pallas kernels for 0% -> 0%
where the time goes in v1:
time: 349 us; the launch traced here: 348 us
  waiting for transfers between devices  143 us (41%)
  Pallas kernels  86.6 us (25%)
  blocking collectives  65.6 us (19%)
  starting transfers between devices  19.5 us (6%)
  between operations  14.4 us (4%)
  local copies, waits for them, and re-layouts  10 us (3%)
  matrix products  6.48 us (2%)
    psum x1, waiting for transfers between devices, body(): lax.psum((partial_sums, partial_counts), ('row', 'col'))  143 us
    pallas_call x1, Pallas kernels, _pair_trunk(): pl.pallas_call(_pair_kernel, out_shape=jax.ShapeDtypeStruct(pair_in.shape...  86.6 us
    psum x1, blocking collectives, body(): lax.psum((partial_sums, partial_counts), ('row', 'col'))  65.6 us
    ppermute x2, starting transfers between devices, with_halo(): lax.ppermute(lax.slice_in_dim(block, 0, width, axis=dim), axis, backward)  11.7 us
    ppermute x2, starting transfers between devices, with_halo(): lax.ppermute(lax.slice_in_dim(block, block.shape[dim] - width, None, axis...  7.75 us
  transfers between devices with their start and end apart: 5, of which 1 were waited for; matrix products, arithmetic and copies ran while one was open for 1% of the time, Pallas kernels for 0%

profile of v1, /device:TPU:1, one launch (start us, length us, event | category | flops | bytes accessed | tf_op | source)
XLA Modules:
  0.0 348.3 jit_solution(17538879143169353249)
XLA Ops:
  7.2 0.9 convert_reduce_fusion.1
  8.3 1.0 convolution_convert_fusion.1
  9.4 1.0 convolution_convert_fusion.2
  10.4 5.7 %collective-permute-start = (bf16[48,256]{1,0:T(8,128)(2,1)S(1)}, bf16[48,256]{1,0:T(8,128)(2,1)S(1)}, u32[]{:S(2)}, u32[]{:S(2)}) collective-permute-start(bf16[48,256]{1,0:T(8,128)(2,1)S(1)} %get-tuple-element.7), channel_id=1, source_target_pairs={{0,1},{1,2},{2,3},{3,4},{4,5},{5,6},{6,7},{7,8},{8,9},{9,10},{10,1... | collective-permute-start | bytes 73736 | tf_op jit(solution)/shard_map/ppermute | solution.py:22
  16.0 4.7 %collective-permute-start.1 = (bf16[48,256]{1,0:T(8,128)(2,1)S(1)}, bf16[48,256]{1,0:T(8,128)(2,1)S(1)}, u32[]{:S(2)}, u32[]{:S(2)}) collective-permute-start(bf16[48,256]{1,0:T(8,128)(2,1)S(1)} %get-tuple-element.8), channel_id=1, source_target_pairs={{1,0},{2,1},{3,2},{4,3},{5,4},{6,5},{7,6},{8,7},{9,8},{10,9},{11,1... | collective-permute-start | bytes 73736 | tf_op jit(solution)/shard_map/ppermute | solution.py:25
  20.8 2.1 collective-permute-start.2
  22.9 7.1 %collective-permute-start.3 = (bf16[48]{0:T(256)(128)(2,1)S(1)}, bf16[48]{0:T(256)(128)(2,1)S(1)}, u32[]{:S(2)}, u32[]{:S(2)}) collective-permute-start(bf16[48]{0:T(256)(128)(2,1)S(1)} %get-tuple-element.12), channel_id=1, source_target_pairs={{1,0},{2,1},{3,2},{4,3},{5,4},{6,5},{7,6},{8,7},{9,8},{10,9},{11,1... | collective-permute-start | bytes 296 | tf_op jit(solution)/shard_map/ppermute | solution.py:25
  30.5 0.5 copy-done.9
  31.2 65.6 %psum.15 = f32[512]{0:T(512)S(1)} all-reduce(f32[512]{0:T(512)S(1)} %convert_reduce_fusion), channel_id=1, replica_groups=mesh['row'=16,'col'=8] {'row','col'}, use_global_device_ids=true, to_apply=%region_7.8 | all-reduce | flops 512 | bytes 4096 | tf_op jit(solution)/shard_map/psum | solution.py:342
  96.9 2.7 gather_fusion.1
  99.8 2.1 gather_fusion
  102.8 0.4 fusion.79
  103.4 0.3 copy-done.8
  103.9 0.6 copy-done.11
  104.5 0.3 fusion.6
  104.9 0.6 copy-done.7
  105.4 1.3 fusion.4
  106.8 143.1 %all-reduce.2.cloned.1.call-done = f32[512,384]{1,0:T(8,128)} async-done(((f32[512,384]{1,0:T(8,128)}), f32[512,384]{1,0:T(8,128)}) %all-reduce.2.cloned.1.call-update) | async-done | bytes 786448 | tf_op jit(solution)/shard_map/psum | solution.py:342
  249.9 1.6 fusion.12
  251.7 0.9 copy-done.1
  252.8 86.6 %pair_trunk.1 = bf16[32,64,128]{2,1,0:T(8,128)(2,1)S(1)} custom-call(bf16[32,64,128]{2,1,0:T(8,128)(2,1)S(1)} %copy-done.1, f32[32,128]{1,0:T(8,128)S(1)} %constant_dynamic-slice_fusion.1.left_ref, f32[64,128]{1,0:T(8,128)S(1)} %constant_dynamic-slice_fusion.right_ref, bf16[6,128,128]{2,1,0:T(8,128)(2,1)S(1)} %copy-done.3, ...), custom_call_target="tpu_custom_call" | custom-call | tf_op jit(solution)/shard_map/pair_trunk/pallas_call | solution.py:239
  339.4 0.6 gather_fusion.2
  340.0 0.7 add_convert_fusion
  340.7 0.8 copy.27
  (64 shorter events, 2.8 us)
Async XLA Ops:
  7.2 242.7 %copy-start = (bf16[384,384]{1,0:T(8,128)(2,1)S(1)}, bf16[384,384]{1,0:T(8,128)(2,1)}, u32[]{:S(2)}) copy-start(bf16[384,384]{1,0:T(8,128)(2,1)} %param.21) | copy-start | bytes 884740
  7.2 0.9 copy-start.6
  7.2 242.7 %all-reduce.2.cloned.1.call-start = ((), (), s32[]{:S(2)}) async-start(), calls=%async_computation | async-start | bytes 1572864 | tf_op jit(solution)/shard_map/psum | solution.py:342
  8.3 21.8 %copy-start.10 = (bf16[5,128,128]{2,1,0:T(8,128)(2,1)S(1)}, bf16[5,128,128]{2,1,0:T(8,128)(2,1)}, u32[]{:S(2)}) copy-start(bf16[5,128,128]{2,1,0:T(8,128)(2,1)} %param.17) | copy-start | bytes 491524
  10.4 10.4 %copy-start.12 = (s32[96]{0:T(128)S(1)}, s32[96]{0:T(128)}, u32[]{:S(2)}) copy-start(s32[96]{0:T(128)} %param.16) | copy-start | bytes 1156
  10.4 89.4 %collective-permute-start = (bf16[48,256]{1,0:T(8,128)(2,1)S(1)}, bf16[48,256]{1,0:T(8,128)(2,1)S(1)}, u32[]{:S(2)}, u32[]{:S(2)}) collective-permute-start(bf16[48,256]{1,0:T(8,128)(2,1)S(1)} %get-tuple-element.7), channel_id=1, source_target_pairs={{0,1},{1,2},{2,3},{3,4},{4,5},{5,6},{6,7},{7,8},{8,9},{9,10},{10,1... | collective-permute-start | bytes 73736 | tf_op jit(solution)/shard_map/ppermute | solution.py:22
  16.0 83.7 %collective-permute-start.1 = (bf16[48,256]{1,0:T(8,128)(2,1)S(1)}, bf16[48,256]{1,0:T(8,128)(2,1)S(1)}, u32[]{:S(2)}, u32[]{:S(2)}) collective-permute-start(bf16[48,256]{1,0:T(8,128)(2,1)S(1)} %get-tuple-element.8), channel_id=1, source_target_pairs={{1,0},{2,1},{3,2},{4,3},{5,4},{6,5},{7,6},{8,7},{9,8},{10,9},{11,1... | collective-permute-start | bytes 73736 | tf_op jit(solution)/shard_map/ppermute | solution.py:25
  20.8 76.0 %collective-permute-start.2 = (bf16[48]{0:T(256)(128)(2,1)S(1)}, bf16[48]{0:T(256)(128)(2,1)S(1)}, u32[]{:S(2)}, u32[]{:S(2)}) collective-permute-start(bf16[48]{0:T(256)(128)(2,1)S(1)} %get-tuple-element.11), channel_id=1, source_target_pairs={{0,1},{1,2},{2,3},{3,4},{4,5},{5,6},{6,7},{7,8},{8,9},{9,10},{10,1... | collective-permute-start | bytes 296 | tf_op jit(solution)/shard_map/ppermute | solution.py:22
  22.9 73.9 %collective-permute-start.3 = (bf16[48]{0:T(256)(128)(2,1)S(1)}, bf16[48]{0:T(256)(128)(2,1)S(1)}, u32[]{:S(2)}, u32[]{:S(2)}) collective-permute-start(bf16[48]{0:T(256)(128)(2,1)S(1)} %get-tuple-element.12), channel_id=1, source_target_pairs={{1,0},{2,1},{3,2},{4,3},{5,4},{6,5},{7,6},{8,7},{9,8},{10,9},{11,1... | collective-permute-start | bytes 296 | tf_op jit(solution)/shard_map/ppermute | solution.py:25
  30.4 0.7 copy-start.9
  102.8 0.9 copy-start.8
  103.7 0.8 copy-start.11
  104.5 0.9 copy-start.7
  251.5 1.0 copy-start.1
  251.5 1.1 copy-start.2
  251.5 1.1 copy-start.3
  251.5 1.2 copy-start.4
  251.5 1.2 copy-start.5
Sparse Core Ops, SparseCore 0:
  106.9 142.9 all-reduce.1

commit v2 on v1

v2 whole, which is shorter than its diff:
```python
import jax
import jax.numpy as jnp
from jax import lax
from jax.experimental import pallas as pl
from jax.experimental.pallas import tpu as pltpu
from jax.sharding import PartitionSpec as P

HEADS = 4
QWIN = 32
KWIN = 128
SIDE = 48
SLOTS = 96
WIDE = SLOTS + 2 * SIDE

epsilon = 1e-05

def _peers(r, c, fn):
    for m in range(1, 128):
        n = (m * 45) % 128
        fn(lax.rem(r + n // 8, 16), lax.rem(c + n % 8, 8))


def _sigmoid(x):
    return 0.5 * jnp.tanh(0.5 * x) + 0.5


def _norm(x):
    center = x - jnp.mean(x, 0, keepdims=True)
    spread = jnp.mean(center * center, 0, keepdims=True)
    return center * lax.rsqrt(spread + epsilon)


def _dot(a, b):
    return jnp.dot(a, b, preferred_element_type=jnp.float32)


def _flip(x):
    return jnp.transpose(x.astype(jnp.float32)).astype(jnp.bfloat16)


def _norm_rows(x):
    center = x - jnp.mean(x, -1, keepdims=True)
    spread = jnp.mean(center * center, -1, keepdims=True)
    return center * lax.rsqrt(spread + epsilon)


def _ones_where(condition):
    return jnp.where(condition, 1.0, 0.0).astype(jnp.bfloat16)


def _kernel(
    pair_ref, atoms_ref, token_ref, mask_ref, atom_w_ref, atom_tin_ref, atom_tout_ref,
    token_in_ref, token_out_ref, out_w_ref, in_w_ref, tin_ref, tout_ref,
    result_ref, atoms_out_ref,
    state, normed, gate, rows32, weights, tin_t, tout_t,
    send_l, send_r, send_p, recv_l, recv_r, recv_p, mat_l, mat_r, mat_p,
    halo_out, halo_in, flags, live_token, any_token, wide, mid, featured,
    send_t, recv_t, share, recv_row, recv_right, left32, right64, add32, recv_add,
    sent, got, entered,
):
    r = lax.axis_index("row")
    c = lax.axis_index("col")
    me = r * 8 + c
    barrier = pltpu.get_barrier_semaphore()
    after = lax.rem(me + 1, 128)
    before = lax.rem(me + 127, 128)

    def greet(semaphore, row, col):
        pl.semaphore_signal(
            semaphore, inc=1, device_id=(row, col), device_id_type=pl.DeviceIdType.MESH
        )

    def copy(source, target, k, row, col):
        pltpu.make_async_remote_copy(
            src_ref=source,
            dst_ref=target,
            send_sem=sent.at[k],
            recv_sem=got.at[k],
            device_id=(row, col),
            device_id_type=pl.DeviceIdType.MESH,
        ).start()

    def await_bytes(ref, semaphore):
        pltpu.make_async_copy(ref, ref, semaphore).wait()

    greet(barrier, after // 8, lax.rem(after, 8))
    greet(barrier, before // 8, lax.rem(before, 8))
    for step in range(1, 8):
        greet(barrier, r, lax.rem(c + step, 8))
    for step in range(1, 16):
        greet(barrier, lax.rem(r + step, 16), c)

    flags[...] = jnp.zeros_like(flags)
    flags[:, :SLOTS] = jnp.broadcast_to(
        jnp.where(mask_ref[...] == 1, 1.0, 0.0), (16, SLOTS)
    )
    any_token[...] = jnp.full_like(any_token, -1)
    any_token[:, :SLOTS] = jnp.broadcast_to(token_ref[...], (8, SLOTS))
    own_flags = flags[...].astype(jnp.bfloat16)
    halo_out[0, :SIDE] = atoms_ref[SLOTS - SIDE :]
    halo_out[1, :SIDE] = atoms_ref[:SIDE]
    halo_out[0, SIDE:] = own_flags
    halo_out[1, SIDE:] = own_flags
    live_token[...] = jnp.where(flags[:8] > 0.5, any_token[...], -1)
    pl.semaphore_wait(barrier, 24)
    copy(halo_out.at[0], halo_in.at[0], 6, after // 8, lax.rem(after, 8))
    copy(halo_out.at[1], halo_in.at[1], 7, before // 8, lax.rem(before, 8))
    for step in range(1, 16):
        greet(entered, lax.rem(r + step, 16), c)

    for w in range(6):
        weights[pl.ds(w * 128, 128), :] = _flip(out_w_ref[w])
        weights[pl.ds((6 + w) * 128, 128), :] = _flip(in_w_ref[w])
    for w in range(2):
        tin_t[pl.ds(w * 512, 512), :] = _flip(tin_ref[w])
    tout_t[...] = _flip(tout_ref[...])

    own = atoms_ref[...].astype(jnp.float32)
    own_normed = _norm_rows(own).astype(jnp.bfloat16)
    wide[SIDE : SIDE + SLOTS] = own_normed
    queries = _dot(own_normed, atom_w_ref[0]).astype(jnp.bfloat16)
    atom_gate = _sigmoid(_dot(own_normed, atom_w_ref[3]))
    for k in (6, 7):
        await_bytes(halo_out.at[k - 6], sent.at[k])
        await_bytes(halo_in.at[k - 6], got.at[k])
    wide[:SIDE] = _norm_rows(halo_in[0, :SIDE].astype(jnp.float32)).astype(jnp.bfloat16)
    wide[SIDE + SLOTS :] = _norm_rows(halo_in[1, :SIDE].astype(jnp.float32)).astype(jnp.bfloat16)
    keys = _dot(wide[...], atom_w_ref[1]).astype(jnp.bfloat16)
    values = _dot(wide[...], atom_w_ref[2]).astype(jnp.bfloat16)
    slot = lax.broadcasted_iota(jnp.int32, (128, WIDE), 0)
    key = lax.broadcasted_iota(jnp.int32, (128, WIDE), 1)
    keep = (
        _dot(halo_in[0, SIDE:], _ones_where((key + SIDE == slot) & (me > 0)))
        + _dot(own_flags, _ones_where(key - SIDE == slot))
        + _dot(halo_in[1, SIDE:], _ones_where((key - SIDE - SLOTS == slot) & (me < 127)))
    )[:1]
    query = lax.broadcasted_iota(jnp.int32, (SLOTS, WIDE), 0)
    key = lax.broadcasted_iota(jnp.int32, (SLOTS, WIDE), 1)
    offset = key - (query // QWIN) * QWIN
    inside = (offset >= 0) & (offset < KWIN)
    allowed = jnp.where(inside & ((keep > 0.5) | (key - SIDE == query)), 1.0, 0.0)
    lane_head = lax.broadcasted_iota(jnp.int32, (SLOTS, 128), 1) // 32
    stacked = jnp.concatenate(
        [jnp.where(lane_head == h, queries.astype(jnp.float32), 0.0) for h in range(HEADS)], 0
    ).astype(jnp.bfloat16)
    scores = (
        lax.dot_general(
            stacked, keys, (((1,), (1,)), ((), ())), preferred_element_type=jnp.float32
        )
        * 32**-0.5
    )
    raw = jnp.where(jnp.concatenate([allowed] * HEADS, 0) > 0.5, jnp.exp(scores), 0.0)
    attention = (raw / jnp.sum(raw, -1, keepdims=True)).astype(jnp.bfloat16)
    spread = _dot(attention, values)
    attended = jnp.zeros((SLOTS, 128), jnp.float32)
    for h in range(HEADS):
        attended = attended + jnp.where(lane_head == h, spread[h * SLOTS : (h + 1) * SLOTS], 0.0)
    gated = (atom_gate * attended).astype(jnp.bfloat16)
    resid = own + _dot(gated, atom_w_ref[4])
    resid_normed = _norm_rows(resid).astype(jnp.bfloat16)
    up = _dot(resid_normed, atom_tin_ref[0])
    hidden = (up * _sigmoid(up) * _dot(resid_normed, atom_tin_ref[1])).astype(jnp.bfloat16)
    atom_mid = resid + _dot(hidden, atom_tout_ref[...])
    mid[...] = atom_mid
    feature = jnp.maximum(_dot(atom_mid.astype(jnp.bfloat16), token_in_ref[...]), 0.0)
    featured[...] = jnp.zeros_like(featured)
    featured[:SLOTS, :384] = feature.astype(jnp.bfloat16)
    featured[:SLOTS, 384:] = jnp.ones((SLOTS, 128), jnp.bfloat16)

    for t in range(4):
        owner = lax.broadcasted_iota(jnp.int32, (128, 128), 0)
        member = _ones_where(owner * 4 + t == live_token[:1])
        sums = _dot(member, featured[...])
        for m in range(4):
            rows32[pl.ds(4 * m + t, 128, stride=16), :] = sums[:, m * 128 : (m + 1) * 128]

    def pack(target):
        def move(d, _):
            target[pl.ds(d * 8, 8)] = (
                rows32[pl.ds(d * 128, 128), :].reshape(8, 16, 128).astype(jnp.bfloat16)
            )
            return 0

        lax.fori_loop(0, 16, move, 0)

    def launch(source, target, k):
        target[me] = source[me]
        _peers(r, c, lambda row, col: copy(source.at[row * 8 + col], target.at[me], k, row, col))

    def finish_copies(source, target, k):
        part = pl.ds(0, 127)
        await_bytes(source.at[part], sent.at[k])
        await_bytes(target.at[part], got.at[k])

    pack(send_t)
    pl.semaphore_wait(entered, 15)
    launch(send_t, recv_t, 8)
    finish_copies(send_t, recv_t, 8)

    def gather_sums(d, total):
        return total + jnp.sum(recv_t[pl.ds(d * 8, 8)].astype(jnp.float32), 0)

    total = lax.fori_loop(0, 16, gather_sums, jnp.zeros((16, 128), jnp.float32))
    count = jnp.maximum(total[12:], 1.0)
    proj = jnp.zeros((4, 384), jnp.float32)
    for m in range(3):
        single = (total[4 * m : 4 * m + 4] / count).astype(jnp.bfloat16)
        proj = proj + _dot(single, token_out_ref[pl.ds(m * 128, 128), :])
    share[...] = jnp.zeros_like(share)
    for m in range(3):
        share[4 * m : 4 * m + 4] = proj[:, m * 128 : (m + 1) * 128]

    recv_row[c] = share[...]
    column = me // 16
    place = lax.rem(me, 16)
    for step in range(1, 8):
        copy(share, recv_row.at[c], 9, r, lax.rem(c + step, 8))
    for step in range(1, 16):
        row = lax.rem(r + step, 16)
        copy(share.at[pl.ds(0, 8)], recv_right.at[place], 10, row, column)

    @pl.when(column == c)
    def _():
        recv_right[place] = share[pl.ds(0, 8)]

    @pl.when(column != c)
    def _():
        copy(share.at[pl.ds(0, 8)], recv_right.at[place], 10, r, column)
        await_bytes(recv_right.at[pl.ds(0, 1)], sent.at[10])
    await_bytes(recv_right.at[pl.ds(0, 15)], sent.at[10])
    await_bytes(recv_row.at[pl.ds(0, 7)], sent.at[9])

    mine = (me >= 16 * c) & (me < 16 * c + 16)

    @pl.when(mine)
    def _():
        await_bytes(recv_right.at[pl.ds(0, 15)], got.at[10])

    @pl.when(jnp.logical_not(mine))
    def _():
        await_bytes(recv_right, got.at[10])

    await_bytes(recv_row.at[pl.ds(0, 7)], got.at[9])
    for j in range(16):
        right64[4 * j : 4 * j + 4] = recv_right[j, 4:8]
    for j in range(8):
        left32[4 * j : 4 * j + 4] = recv_row[j, :4]
        add32[4 * j : 4 * j + 4] = recv_row[j, 8:12]
    recv_add[r] = add32[...]
    for step in range(1, 16):
        copy(add32, recv_add.at[r], 11, lax.rem(r + step, 16), c)

    def start_state(a, _):
        natural = jnp.concatenate([pair_ref[a], pair_ref[a + 16]], 0).astype(jnp.float32)
        right = right64[...]
        natural = natural + jnp.concatenate(
            [right + left32[pl.ds(a, 1), :], right + left32[pl.ds(a + 16, 1), :]], 0
        )
        turned = jnp.transpose(natural)
        state[a] = turned
        normed[a] = _norm(turned).astype(jnp.bfloat16)
        return 0

    lax.fori_loop(0, 16, start_state, 0)

    def edges(base, first):
        def chunk(a, _):
            both = _dot(weights[pl.ds((base + first) * 128, 256), :], normed[a])
            rows32[pl.ds(a, 128, stride=16), :] = _sigmoid(both[:128]) * both[128:]
            return 0

        lax.fori_loop(0, 16, chunk, 0)

    def gates(base):
        def chunk(a, _):
            gate[a] = _sigmoid(_dot(weights[pl.ds((base + 4) * 128, 128), :], normed[a]))
            return 0

        lax.fori_loop(0, 16, chunk, 0)

    def assemble(source, target):
        def block(row, _):
            for q in range(4):
                even = source[row * 8 + 2 * q]
                odd = source[row * 8 + 2 * q + 1]
                target[pl.ds(row * 32, 16), pl.ds(q * 128, 128)] = jnp.concatenate(
                    [even[:, :64], odd[:, :64]], 1
                )
                target[pl.ds(row * 32 + 16, 16), pl.ds(q * 128, 128)] = jnp.concatenate(
                    [even[:, 64:], odd[:, 64:]], 1
                )
            return 0

        lax.fori_loop(0, 16, block, 0)

    def split(source, target):
        def block(row, _):
            for q in range(4):
                top = source[pl.ds(row * 32, 16), pl.ds(q * 128, 128)]
                low = source[pl.ds(row * 32 + 16, 16), pl.ds(q * 128, 128)]
                target[row * 8 + 2 * q] = jnp.concatenate([top[:, :64], low[:, :64]], 1)
                target[row * 8 + 2 * q + 1] = jnp.concatenate([top[:, 64:], low[:, 64:]], 1)
            return 0

        lax.fori_loop(0, 16, block, 0)

    def triangle(t, after):
        base = 6 * t
        edges(base, 0)
        pack(send_l.at[t])
        launch(send_l.at[t], recv_l.at[t], 3 * t)
        edges(base, 2)
        pack(send_r.at[t])
        launch(send_r.at[t], recv_r.at[t], 3 * t + 1)
        gates(base)
        finish_copies(send_l.at[t], recv_l.at[t], 3 * t)
        assemble(recv_l.at[t], mat_l)
        finish_copies(send_r.at[t], recv_r.at[t], 3 * t + 1)
        assemble(recv_r.at[t], mat_r)
        axis = 1 - t
        mat_p[...] = lax.dot_general(
            mat_l[...],
            mat_r[...],
            (((axis,), (axis,)), ((), ())),
            preferred_element_type=jnp.float32,
        ).astype(jnp.bfloat16)
        split(mat_p, send_p.at[t])
        launch(send_p.at[t], recv_p.at[t], 3 * t + 2)
        finish_copies(send_p.at[t], recv_p.at[t], 3 * t + 2)

        def widen(d, _):
            rows32[pl.ds(d * 128, 128), :] = (
                recv_p[t, pl.ds(d * 8, 8)].astype(jnp.float32).reshape(128, 128)
            )
            return 0

        lax.fori_loop(0, 16, widen, 0)

        def close(a, _):
            product = _norm(rows32[pl.ds(a, 128, stride=16), :]).astype(jnp.bfloat16)
            updated = state[a] + gate[a] * _dot(weights[pl.ds((base + 5) * 128, 128), :], product)
            state[a] = updated
            normed[a] = _norm(updated).astype(jnp.bfloat16)
            if after is not None:
                after(a, updated)
            return 0

        lax.fori_loop(0, 16, close, 0)

    def transition(a, updated):
        inner = _dot(tin_t[...], normed[a])
        up = inner[:512]
        hidden = (up * _sigmoid(up) * inner[512:]).astype(jnp.bfloat16)
        final = jnp.transpose(updated + _dot(tout_t[...], hidden)).astype(jnp.bfloat16)
        result_ref[a] = final[:64]
        result_ref[a + 16] = final[64:]

    triangle(0, None)
    triangle(1, transition)

    await_bytes(recv_add.at[pl.ds(0, 15)], sent.at[11])
    await_bytes(recv_add.at[pl.ds(0, 15)], got.at[11])
    added = recv_add[...].reshape(512, 128)
    high = added.astype(jnp.bfloat16)
    low = (added - high.astype(jnp.float32)).astype(jnp.bfloat16)
    token = lax.broadcasted_iota(jnp.int32, (512, 128), 0)
    chosen = _ones_where(token == any_token[:1])
    over = (((0,), (0,)), ((), ()))
    picked = lax.dot_general(
        chosen, high, over, preferred_element_type=jnp.float32
    ) + lax.dot_general(chosen, low, over, preferred_element_type=jnp.float32)
    atoms_out_ref[...] = (mid[...] + picked[:SLOTS]).astype(jnp.bfloat16)


def body(pair_in, atoms_in, atom_token, atom_mask, *parameters):
    vmem = pl.BlockSpec(memory_space=pltpu.VMEM)
    bf16, f32 = jnp.bfloat16, jnp.float32
    message = (2, 128, 16, 128)
    return pl.pallas_call(
        _kernel,
        out_shape=(
            jax.ShapeDtypeStruct(pair_in.shape, bf16),
            jax.ShapeDtypeStruct(atoms_in.shape, bf16),
        ),
        in_specs=[vmem] * 13,
        out_specs=(vmem, vmem),
        scratch_shapes=[
            pltpu.VMEM((16, 128, 128), f32),
            pltpu.VMEM((16, 128, 128), bf16),
            pltpu.VMEM((16, 128, 128), f32),
            pltpu.VMEM((2048, 128), f32),
            pltpu.VMEM((1536, 128), bf16),
            pltpu.VMEM((1024, 128), bf16),
            pltpu.VMEM((128, 512), bf16),
        ]
        + [pltpu.VMEM(message, bf16)] * 6
        + [pltpu.VMEM((512, 512), bf16)] * 3
        + [
            pltpu.VMEM((2, 64, 128), bf16),
            pltpu.VMEM((2, 64, 128), bf16),
            pltpu.VMEM((16, 128), f32),
            pltpu.VMEM((8, 128), jnp.int32),
            pltpu.VMEM((8, 128), jnp.int32),
            pltpu.VMEM((WIDE, 128), bf16),
            pltpu.VMEM((SLOTS, 128), f32),
            pltpu.VMEM((128, 512), bf16),
            pltpu.VMEM((128, 16, 128), bf16),
            pltpu.VMEM((128, 16, 128), bf16),
            pltpu.VMEM((16, 128), f32),
            pltpu.VMEM((8, 16, 128), f32),
            pltpu.VMEM((16, 8, 128), f32),
            pltpu.VMEM((32, 128), f32),
            pltpu.VMEM((64, 128), f32),
            pltpu.VMEM((32, 128), f32),
            pltpu.VMEM((16, 32, 128), f32),
            pltpu.SemaphoreType.DMA((12,)),
            pltpu.SemaphoreType.DMA((12,)),
            pltpu.SemaphoreType.REGULAR,
        ],
        compiler_params=pltpu.CompilerParams(
            collective_id=0, has_side_effects=True, vmem_limit_bytes=48 * 1024 * 1024
        ),
        name="atoms_and_pair",
    )(pair_in, atoms_in, atom_token.reshape(1, SLOTS), atom_mask.reshape(1, SLOTS), *parameters)


def solution(mesh):
    placed = (
        P("row", "col", None),
        P(("row", "col"), None),
        P(("row", "col")),
        P(("row", "col")),
        P(),
        P(),
        P(),
        P(),
        P(),
        P(),
        P(),
        P(),
        P(),
    )
    return jax.shard_map(
        body,
        mesh=mesh,
        in_specs=placed,
        out_specs=(P("row", "col", None), P(("row", "col"), None)),
        check_vma=False,
    )
```

time: 349 us -> 128 us (0.37)
  waiting for transfers between devices: 143 us -> 0 us
  blocking collectives: 65.6 us -> 0 us
  Pallas kernels: 86.6 us -> 115 us
  starting transfers between devices: 19.5 us -> 0 us
  between operations: 14.4 us -> 0.67 us
  matrix products: 6.48 us -> 0 us
    psum x1 -> x0, waiting for transfers between devices: 143 us -> none  [body(): lax.psum((partial_sums, partial_counts), ('row', 'col'))]
    psum x1 -> x0, blocking collectives: 65.6 us -> none  [body(): lax.psum((partial_sums, partial_counts), ('row', 'col'))]
    pallas_call x1, Pallas kernels: 86.6 us -> 115 us  [body(): pl.pallas_call(_kernel, out_shape=(jax.ShapeDtypeStruct(pair_in.shape, bf...]
    ppermute x4 -> x0, starting transfers between devices: 19.5 us -> none  [the longest x2 11.7 us: with_halo(): lax.ppermute(lax.slice_in_dim(block, 0, width, axis=dim), axis, backward)]
    unnamed x27 -> x28, local copies, waits for them, and re-layouts: 3.95 us -> 12.1 us
    dot_general x10 -> x0, matrix products: 6.48 us -> none  [the longest x6 3.15 us: linear(): jnp.einsum('...k,kn->...n', inputs, weight, preferred_element_type=jnp.fl...]
    gather x4 -> x0, local copies, waits for them, and re-layouts: 5.53 us -> none  [the longest x1 2.69 us: attend(): window_keep = jnp.take(wide_keep, key_index, axis=0)]
  transfers between devices with their start and end apart: 5 -> 0, of which waited for: 1 -> 0; matrix products, arithmetic and copies ran while one was open for 1% -> 0% of each run, Pallas kernels for 0% -> 0%
where the time goes in v2:
time: 128 us; the launch traced here: 127 us
  Pallas kernels  115 us (90%)
  local copies, waits for them, and re-layouts  12.1 us (9%)
    pallas_call x1, Pallas kernels, body(): pl.pallas_call(_kernel, out_shape=(jax.ShapeDtypeStruct(pair_in.shape, bf...  115 us
    unnamed x28, local copies, waits for them, and re-layouts  12.1 us

profile of v2, /device:TPU:1, one launch (start us, length us, event | category | flops | bytes accessed | tf_op | source)
XLA Modules:
  0.0 127.2 jit_solution(5192469649890805736)
XLA Ops:
  0.6 0.0 copy-start.11
  0.6 0.0 copy-start.12
  0.7 0.6 copy-done.11
  1.3 0.0 copy-done.12
  1.3 0.0 copy-start
  1.3 1.0 copy-done
  2.3 0.0 copy-start.1
  2.4 1.0 copy-done.1
  3.3 0.0 copy-start.2
  3.3 0.9 copy-done.2
  4.3 0.0 copy-start.3
  4.3 0.9 copy-done.3
  5.2 0.0 copy-start.4
  5.2 0.9 copy-done.4
  6.1 0.0 copy-start.5
  6.1 0.9 copy-done.5
  7.0 0.9 copy-done.6
  7.9 0.9 copy-done.7
  8.8 0.9 copy-done.8
  9.7 0.8 copy-done.9
  10.6 0.7 copy-done.10
  11.3 114.5 %atoms_and_pair.1 = (bf16[32,64,128]{2,1,0:T(8,128)(2,1)S(1)}, bf16[96,128]{1,0:T(8,128)(2,1)S(1)}) custom-call(bf16[32,64,128]{2,1,0:T(8,128)(2,1)S(1)} %copy-done, bf16[96,128]{1,0:T(8,128)(2,1)S(1)} %copy-done.10, s32[1,96]{1,0:T(1,128)S(1)} %bitcast.2, s32[1,96]{1,0:T(1,128)S(1)} %bitcast.3, bf16[5,128,128]{2,1,0:T(8,128)(2,1)S(1)} %copy-done.5, ...), custom_call_target="tpu_custom_call" | custom-call | tf_op jit(solution)/shard_map/atoms_and_pair/pallas_call | solution.py:379
  125.8 0.8 copy.17
  126.6 0.6 copy.18
  (5 shorter events, 0.0 us)
Async XLA Ops:
  0.6 0.7 copy-start.11
  0.6 0.7 copy-start.12
  1.3 1.0 copy-start
  2.3 1.0 copy-start.1
  3.3 0.9 copy-start.2
  4.3 0.9 copy-start.3
  5.2 0.9 copy-start.4
  6.1 0.9 copy-start.5
  7.0 0.9 copy-start.6
  7.9 0.9 copy-start.7
  8.8 0.9 copy-start.8
  9.7 0.8 copy-start.9
  10.6 0.7 copy-start.10

commit v3 on v2

--- a/solution.py
+++ b/solution.py
@@ -11,13 +11,33 @@
 SIDE = 48
 SLOTS = 96
 WIDE = SLOTS + 2 * SIDE
+START = 512
+EDGE = 2048
+CLOSE = 512
+LAST = 1024
+ROWS = 16
 
 epsilon = 1e-05
 
-def _peers(r, c, fn):
-    for m in range(1, 128):
-        n = (m * 45) % 128
-        fn(lax.rem(r + n // 8, 16), lax.rem(c + n % 8, 8))
+def _far_first():
+    shifts = [
+        (x, y, z, core) for x in range(4) for y in range(4) for z in range(4) for core in range(2)
+    ][1:]
+    return sorted(shifts, key=lambda shift: -sum(min(s, 4 - s) for s in shift[:3]))
+
+
+def _peers(r, c):
+    z, y, core, x = r // 4, lax.rem(c, 2) * 2 + lax.rem(r // 2, 2), lax.rem(r, 2), c // 2
+    col_x = [lax.rem(x + s, 4) * 2 for s in range(4)]
+    ys = [lax.rem(y + s, 4) for s in range(4)]
+    col_y = [s // 2 for s in ys]
+    row_y = [lax.rem(s, 2) * 2 for s in ys]
+    row_z = [lax.rem(z + s, 4) * 4 for s in range(4)]
+    cores = [core, 1 - core]
+    return [
+        (row_z[dz] + row_y[dy] + cores[dcore], col_x[dx] + col_y[dy])
+        for dx, dy, dz, dcore in _far_first()
+    ]
 
 
 def _sigmoid(x):
@@ -49,18 +69,22 @@
 
 
 def _kernel(
-    pair_ref, atoms_ref, token_ref, mask_ref, atom_w_ref, atom_tin_ref, atom_tout_ref,
-    token_in_ref, token_out_ref, out_w_ref, in_w_ref, tin_ref, tout_ref,
-    result_ref, atoms_out_ref,
-    state, normed, gate, rows32, weights, tin_t, tout_t,
+    token_ref, mask_ref, *refs,
+):
+    sources, refs = refs[:11], refs[11:]
+    result_ref, atoms_out_ref, *refs = refs
+    staged, refs = refs[:11], refs[11:]
+    (pair_ref, atoms_ref, atom_w_ref, atom_tin_ref, atom_tout_ref,
+     token_in_ref, token_out_ref, out_w_ref, in_w_ref, tin_ref, tout_ref) = staged
+    (    state, normed, gate, rows32, weights, tin_t, tout_t,
     send_l, send_r, send_p, recv_l, recv_r, recv_p, mat_l, mat_r, mat_p,
     halo_out, halo_in, flags, live_token, any_token, wide, mid, featured,
     send_t, recv_t, share, recv_row, recv_right, left32, right64, add32, recv_add,
-    sent, got, entered,
-):
+    sent, got, entered, loaded) = refs
     r = lax.axis_index("row")
     c = lax.axis_index("col")
     me = r * 8 + c
+    peers = _peers(r, c)
     barrier = pltpu.get_barrier_semaphore()
     after = lax.rem(me + 1, 128)
     before = lax.rem(me + 127, 128)
@@ -90,6 +114,13 @@
     for step in range(1, 16):
         greet(barrier, lax.rem(r + step, 16), c)
 
+    loads = [
+        pltpu.make_async_copy(source, place, loaded.at[k])
+        for k, (source, place) in enumerate(zip(sources, staged))
+    ]
+    for k in (1, 2, 3, 4, 5, 6, 0, 7, 8, 9, 10):
+        loads[k].start()
+
     flags[...] = jnp.zeros_like(flags)
     flags[:, :SLOTS] = jnp.broadcast_to(
         jnp.where(mask_ref[...] == 1, 1.0, 0.0), (16, SLOTS)
@@ -97,6 +128,7 @@
     any_token[...] = jnp.full_like(any_token, -1)
     any_token[:, :SLOTS] = jnp.broadcast_to(token_ref[...], (8, SLOTS))
     own_flags = flags[...].astype(jnp.bfloat16)
+    loads[1].wait()
     halo_out[0, :SIDE] = atoms_ref[SLOTS - SIDE :]
     halo_out[1, :SIDE] = atoms_ref[:SIDE]
     halo_out[0, SIDE:] = own_flags
@@ -108,6 +140,8 @@
     for step in range(1, 16):
         greet(entered, lax.rem(r + step, 16), c)
 
+    for k in range(7, 11):
+        loads[k].wait()
     for w in range(6):
         weights[pl.ds(w * 128, 128), :] = _flip(out_w_ref[w])
         weights[pl.ds((6 + w) * 128, 128), :] = _flip(in_w_ref[w])
@@ -118,6 +152,7 @@
     own = atoms_ref[...].astype(jnp.float32)
     own_normed = _norm_rows(own).astype(jnp.bfloat16)
     wide[SIDE : SIDE + SLOTS] = own_normed
+    loads[2].wait()
     queries = _dot(own_normed, atom_w_ref[0]).astype(jnp.bfloat16)
     atom_gate = _sigmoid(_dot(own_normed, atom_w_ref[3]))
     for k in (6, 7):
@@ -158,6 +193,8 @@
     gated = (atom_gate * attended).astype(jnp.bfloat16)
     resid = own + _dot(gated, atom_w_ref[4])
     resid_normed = _norm_rows(resid).astype(jnp.bfloat16)
+    for k in (3, 4, 5):
+        loads[k].wait()
     up = _dot(resid_normed, atom_tin_ref[0])
     hidden = (up * _sigmoid(up) * _dot(resid_normed, atom_tin_ref[1])).astype(jnp.bfloat16)
     atom_mid = resid + _dot(hidden, atom_tout_ref[...])
@@ -185,7 +222,8 @@
 
     def launch(source, target, k):
         target[me] = source[me]
-        _peers(r, c, lambda row, col: copy(source.at[row * 8 + col], target.at[me], k, row, col))
+        for row, col in peers:
+            copy(source.at[row * 8 + col], target.at[me], k, row, col)
 
     def finish_copies(source, target, k):
         part = pl.ds(0, 127)
@@ -201,6 +239,7 @@
         return total + jnp.sum(recv_t[pl.ds(d * 8, 8)].astype(jnp.float32), 0)
 
     total = lax.fori_loop(0, 16, gather_sums, jnp.zeros((16, 128), jnp.float32))
+    loads[6].wait()
     count = jnp.maximum(total[12:], 1.0)
     proj = jnp.zeros((4, 384), jnp.float32)
     for m in range(3):
@@ -250,61 +289,83 @@
     for step in range(1, 16):
         copy(add32, recv_add.at[r], 11, lax.rem(r + step, 16), c)
 
-    def start_state(a, _):
-        natural = jnp.concatenate([pair_ref[a], pair_ref[a + 16]], 0).astype(jnp.float32)
+    loads[0].wait()
+
+    def spans(width, step):
+        if width == 2048:
+            step(0)
+        else:
+            lax.fori_loop(0, 2048 // width, lambda g, _: (step(g), 0)[1], 0)
+
+    def lanes(g, width):
+        return pl.ds(g * width if isinstance(g, int) else pl.multiple_of(g * width, width), width)
+
+    def start_state(g):
         right = right64[...]
-        natural = natural + jnp.concatenate(
-            [right + left32[pl.ds(a, 1), :], right + left32[pl.ds(a + 16, 1), :]], 0
-        )
-        turned = jnp.transpose(natural)
-        state[a] = turned
-        normed[a] = _norm(turned).astype(jnp.bfloat16)
-        return 0
-
-    lax.fori_loop(0, 16, start_state, 0)
+        for h in range(START // 128):
+            a = g * (START // 128) + h
+            natural = jnp.concatenate([pair_ref[a], pair_ref[a + 16]], 0).astype(jnp.float32)
+            natural = natural + jnp.concatenate(
+                [right + left32[pl.ds(a, 1), :], right + left32[pl.ds(a + 16, 1), :]], 0
+            )
+            turned = jnp.transpose(natural)
+            state[:, lanes(a, 128)] = turned
+            normed[:, lanes(a, 128)] = _norm(turned).astype(jnp.bfloat16)
+
+    spans(START, start_state)
 
     def edges(base, first):
-        def chunk(a, _):
-            both = _dot(weights[pl.ds((base + first) * 128, 256), :], normed[a])
-            rows32[pl.ds(a, 128, stride=16), :] = _sigmoid(both[:128]) * both[128:]
+        def chunk(g):
+            both = _dot(weights[pl.ds((base + first) * 128, 256), :], normed[:, lanes(g, EDGE)])
+            edge = _sigmoid(both[:128]) * both[128:]
+            for h in range(EDGE // 128):
+                rows32[pl.ds(g * (EDGE // 128) + h, 128, stride=16), :] = edge[
+                    :, h * 128 : (h + 1) * 128
+                ]
+
+        spans(EDGE, chunk)
+
+    def gates(base):
+        def chunk(g):
+            gate[:, lanes(g, EDGE)] = _sigmoid(
+                _dot(weights[pl.ds((base + 4) * 128, 128), :], normed[:, lanes(g, EDGE)])
+            )
+
+        spans(EDGE, chunk)
+
+    low_lanes = lax.broadcasted_iota(jnp.int32, (16, 128), 1) < 64
+
+    def assemble(source, target):
+        def block(g, _):
+            for k in range(ROWS):
+                row = g * ROWS + k
+                for q in range(4):
+                    even = source[row * 8 + 2 * q]
+                    odd = source[row * 8 + 2 * q + 1]
+                    target[pl.ds(row * 32, 16), pl.ds(q * 128, 128)] = jnp.where(
+                        low_lanes, even, pltpu.roll(odd, 64, 1)
+                    )
+                    target[pl.ds(row * 32 + 16, 16), pl.ds(q * 128, 128)] = jnp.where(
+                        low_lanes, pltpu.roll(even, 64, 1), odd
+                    )
             return 0
 
-        lax.fori_loop(0, 16, chunk, 0)
-
-    def gates(base):
-        def chunk(a, _):
-            gate[a] = _sigmoid(_dot(weights[pl.ds((base + 4) * 128, 128), :], normed[a]))
+        lax.fori_loop(0, 16 // ROWS, block, 0)
+
+    def split(source, target):
+        def block(g, _):
+            for k in range(ROWS):
+                row = g * ROWS + k
+                for q in range(4):
+                    top = source[pl.ds(row * 32, 16), pl.ds(q * 128, 128)]
+                    low = source[pl.ds(row * 32 + 16, 16), pl.ds(q * 128, 128)]
+                    target[row * 8 + 2 * q] = jnp.where(low_lanes, top, pltpu.roll(low, 64, 1))
+                    target[row * 8 + 2 * q + 1] = jnp.where(low_lanes, pltpu.roll(top, 64, 1), low)
             return 0
 
-        lax.fori_loop(0, 16, chunk, 0)
-
-    def assemble(source, target):
-        def block(row, _):
-            for q in range(4):
-                even = source[row * 8 + 2 * q]
-                odd = source[row * 8 + 2 * q + 1]
-                target[pl.ds(row * 32, 16), pl.ds(q * 128, 128)] = jnp.concatenate(
-                    [even[:, :64], odd[:, :64]], 1
-                )
-                target[pl.ds(row * 32 + 16, 16), pl.ds(q * 128, 128)] = jnp.concatenate(
-                    [even[:, 64:], odd[:, 64:]], 1
-                )
-            return 0
-
-        lax.fori_loop(0, 16, block, 0)
-
-    def split(source, target):
-        def block(row, _):
-            for q in range(4):
-                top = source[pl.ds(row * 32, 16), pl.ds(q * 128, 128)]
-                low = source[pl.ds(row * 32 + 16, 16), pl.ds(q * 128, 128)]
-                target[row * 8 + 2 * q] = jnp.concatenate([top[:, :64], low[:, :64]], 1)
-                target[row * 8 + 2 * q + 1] = jnp.concatenate([top[:, 64:], low[:, 64:]], 1)
-            return 0
-
-        lax.fori_loop(0, 16, block, 0)
-
-    def triangle(t, after):
+        lax.fori_loop(0, 16 // ROWS, block, 0)
+
+    def triangle(t, width, after):
         base = 6 * t
         edges(base, 0)
         pack(send_l.at[t])
@@ -336,27 +397,36 @@
 
         lax.fori_loop(0, 16, widen, 0)
 
-        def close(a, _):
-            product = _norm(rows32[pl.ds(a, 128, stride=16), :]).astype(jnp.bfloat16)
-            updated = state[a] + gate[a] * _dot(weights[pl.ds((base + 5) * 128, 128), :], product)
-            state[a] = updated
-            normed[a] = _norm(updated).astype(jnp.bfloat16)
-            if after is not None:
-                after(a, updated)
-            return 0
-
-        lax.fori_loop(0, 16, close, 0)
-
-    def transition(a, updated):
-        inner = _dot(tin_t[...], normed[a])
+        def close(g):
+            count = width // 128
+            product = jnp.concatenate(
+                [rows32[pl.ds(g * count + h, 128, stride=16), :] for h in range(count)], 1
+            )
+            product = _norm(product).astype(jnp.bfloat16)
+            here = lanes(g, width)
+            updated = state[:, here] + gate[:, here] * _dot(
+                weights[pl.ds((base + 5) * 128, 128), :], product
+            )
+            after(g, width, updated)
+
+        spans(width, close)
+
+    def next_update(g, width, updated):
+        state[:, lanes(g, width)] = updated
+        normed[:, lanes(g, width)] = _norm(updated).astype(jnp.bfloat16)
+
+    def transition(g, width, updated):
+        inner = _dot(tin_t[...], _norm(updated).astype(jnp.bfloat16))
         up = inner[:512]
         hidden = (up * _sigmoid(up) * inner[512:]).astype(jnp.bfloat16)
-        final = jnp.transpose(updated + _dot(tout_t[...], hidden)).astype(jnp.bfloat16)
-        result_ref[a] = final[:64]
-        result_ref[a + 16] = final[64:]
-
-    triangle(0, None)
-    triangle(1, transition)
+        final = updated + _dot(tout_t[...], hidden)
+        for h in range(width // 128):
+            natural = jnp.transpose(final[:, h * 128 : (h + 1) * 128]).astype(jnp.bfloat16)
+            result_ref[g * (width // 128) + h] = natural[:64]
+            result_ref[g * (width // 128) + h + 16] = natural[64:]
+
+    triangle(0, CLOSE, next_update)
+    triangle(1, LAST, transition)
 
     await_bytes(recv_add.at[pl.ds(0, 15)], sent.at[11])
     await_bytes(recv_add.at[pl.ds(0, 15)], got.at[11])
@@ -374,6 +444,7 @@
 
 def body(pair_in, atoms_in, atom_token, atom_mask, *parameters):
     vmem = pl.BlockSpec(memory_space=pltpu.VMEM)
+    staged = (pair_in, atoms_in, *parameters)
     bf16, f32 = jnp.bfloat16, jnp.float32
     message = (2, 128, 16, 128)
     return pl.pallas_call(
@@ -382,12 +453,13 @@
             jax.ShapeDtypeStruct(pair_in.shape, bf16),
             jax.ShapeDtypeStruct(atoms_in.shape, bf16),
         ),
-        in_specs=[vmem] * 13,
+        in_specs=[vmem] * 2 + [pl.BlockSpec(memory_space=pltpu.HBM)] * 11,
         out_specs=(vmem, vmem),
-        scratch_shapes=[
-            pltpu.VMEM((16, 128, 128), f32),
-            pltpu.VMEM((16, 128, 128), bf16),
-            pltpu.VMEM((16, 128, 128), f32),
+        scratch_shapes=[pltpu.VMEM(array.shape, array.dtype) for array in staged]
+        + [
+            pltpu.VMEM((128, 2048), f32),
+            pltpu.VMEM((128, 2048), bf16),
+            pltpu.VMEM((128, 2048), f32),
             pltpu.VMEM((2048, 128), f32),
             pltpu.VMEM((1536, 128), bf16),
             pltpu.VMEM((1024, 128), bf16),
@@ -416,12 +488,13 @@
             pltpu.SemaphoreType.DMA((12,)),
             pltpu.SemaphoreType.DMA((12,)),
             pltpu.SemaphoreType.REGULAR,
+            pltpu.SemaphoreType.DMA((11,)),
         ],
         compiler_params=pltpu.CompilerParams(
-            collective_id=0, has_side_effects=True, vmem_limit_bytes=48 * 1024 * 1024
+            collective_id=0, has_side_effects=True, vmem_limit_bytes=60 * 1024 * 1024
         ),
         name="atoms_and_pair",
-    )(pair_in, atoms_in, atom_token.reshape(1, SLOTS), atom_mask.reshape(1, SLOTS), *parameters)
+    )(atom_token.reshape(1, SLOTS), atom_mask.reshape(1, SLOTS), *staged)
 
 
 def solution(mesh):

time: 128 us -> 93.1 us (0.73)
  Pallas kernels: 115 us -> 89.8 us
  local copies, waits for them, and re-layouts: 12.1 us -> 2.49 us
    pallas_call x1, Pallas kernels: 115 us -> 89.8 us  [body(): pl.pallas_call(_kernel, out_shape=(jax.ShapeDtypeStruct(pair_in.shape, bf...]
    unnamed x28 -> x4, local copies, waits for them, and re-layouts: 12.1 us -> 2.49 us
where the time goes in v3:
time: 93.1 us; the launch traced here: 93 us
  Pallas kernels  89.8 us (96%)
  local copies, waits for them, and re-layouts  2.49 us (3%)
    pallas_call x1, Pallas kernels, body(): pl.pallas_call(_kernel, out_shape=(jax.ShapeDtypeStruct(pair_in.shape, bf...  89.8 us
    unnamed x4, local copies, waits for them, and re-layouts  2.49 us

profile of v3, /device:TPU:1, one launch (start us, length us, event | category | flops | bytes accessed | tf_op | source)
XLA Modules:
  0.0 93.0 jit_solution(3351293173989221937)
XLA Ops:
  0.6 89.8 %atoms_and_pair.1 = (bf16[32,64,128]{2,1,0:T(8,128)(2,1)}, bf16[96,128]{1,0:T(8,128)(2,1)}) custom-call(s32[1,96]{1,0:T(1,128)} %bitcast.2, s32[1,96]{1,0:T(1,128)} %bitcast.3, bf16[32,64,128]{2,1,0:T(8,128)(2,1)} %refs_0_.1, bf16[96,128]{1,0:T(8,128)(2,1)} %refs_1_.1, bf16[5,128,128]{2,1,0:T(8,128)(2,1)} %refs_2_.1, bf16[2,128,256]{2,1,0:T(8,128)(2,1)} %refs_3_.1, ...), custom_call_target="tpu_custom_call" | custom-call | tf_op jit(solution)/shard_map/atoms_and_pair/pallas_call | solution.py:450
  90.5 0.0 copy-start
  90.5 1.9 %copy.17 = bf16[32,64,128]{2,1,0:T(8,128)(2,1)} copy(bf16[32,64,128]{2,1,0:T(8,128)(2,1)} %get-tuple-element.4) | data formatting | bytes 1048576
  92.4 0.0 copy-done
  92.4 0.6 copy.18
Async XLA Ops:
  90.5 1.9 %copy-start = (bf16[96,128]{1,0:T(8,128)(2,1)S(1)}, bf16[96,128]{1,0:T(8,128)(2,1)}, u32[]{:S(2)}) copy-start(bf16[96,128]{1,0:T(8,128)(2,1)} %get-tuple-element.5) | copy-start | bytes 73732

commit v4 on v3

--- a/solution.py
+++ b/solution.py
@@ -11,33 +11,31 @@
 SIDE = 48
 SLOTS = 96
 WIDE = SLOTS + 2 * SIDE
-START = 512
+START = 2048
 EDGE = 2048
-CLOSE = 512
+CLOSE = 2048
 LAST = 1024
 ROWS = 16
 
 epsilon = 1e-05
 
 def _far_first():
-    shifts = [
-        (x, y, z, core) for x in range(4) for y in range(4) for z in range(4) for core in range(2)
-    ][1:]
-    return sorted(shifts, key=lambda shift: -sum(min(s, 4 - s) for s in shift[:3]))
-
-
-def _peers(r, c):
-    z, y, core, x = r // 4, lax.rem(c, 2) * 2 + lax.rem(r // 2, 2), lax.rem(r, 2), c // 2
-    col_x = [lax.rem(x + s, 4) * 2 for s in range(4)]
-    ys = [lax.rem(y + s, 4) for s in range(4)]
-    col_y = [s // 2 for s in ys]
-    row_y = [lax.rem(s, 2) * 2 for s in ys]
-    row_z = [lax.rem(z + s, 4) * 4 for s in range(4)]
-    cores = [core, 1 - core]
-    return [
-        (row_z[dz] + row_y[dy] + cores[dcore], col_x[dx] + col_y[dy])
-        for dx, dy, dz, dcore in _far_first()
-    ]
+    shifts = [(x, y, z) for x in range(4) for y in range(4) for z in range(4)][1:]
+    return sorted(shifts, key=lambda shift: -sum(min(s, 4 - s) for s in shift))
+
+
+def _chips(r, c):
+    z, y, x = r // 4, lax.rem(c, 2) * 2 + lax.rem(r // 2, 2), c // 2
+    xs, ys, zs = [[lax.rem(v + s, 4) for s in range(4)] for v in (x, y, z)]
+    row_y = [lax.rem(v, 2) * 2 for v in ys]
+    col_y = [v // 2 for v in ys]
+
+    def chip(dx, dy, dz):
+        row = zs[dz] * 4 + row_y[dy]
+        return row, xs[dx] * 2 + col_y[dy], xs[dx] * 8 + ys[dy] * 2 + zs[dz] // 2
+
+    others = [chip(*shift) + (sum(shift) % 2,) for shift in _far_first()]
+    return chip(0, 0, 0)[2], lax.rem(x + y + z, 2), others
 
 
 def _sigmoid(x):
@@ -77,14 +75,18 @@
     (pair_ref, atoms_ref, atom_w_ref, atom_tin_ref, atom_tout_ref,
      token_in_ref, token_out_ref, out_w_ref, in_w_ref, tin_ref, tout_ref) = staged
     (    state, normed, gate, rows32, weights, tin_t, tout_t,
-    send_l, send_r, send_p, recv_l, recv_r, recv_p, mat_l, mat_r, mat_p,
+    send_e, recv_e, edge32, send_p, recv_p, mat_l, mat_r, mat_p,
     halo_out, halo_in, flags, live_token, any_token, wide, mid, featured,
-    send_t, recv_t, share, recv_row, recv_right, left32, right64, add32, recv_add,
+    send_t, recv_t, share, recv_row, recv_right, spreader, add32, recv_add,
     sent, got, entered, loaded) = refs
     r = lax.axis_index("row")
     c = lax.axis_index("col")
     me = r * 8 + c
-    peers = _peers(r, c)
+    spot, parity, chips = _chips(r, c)
+    core = lax.rem(r, 2)
+    sibling = r + 1 - 2 * core
+    channel = core * 64 + parity * 32 + spot
+    sibling_channel = (1 - core) * 64 + parity * 32 + spot
     barrier = pltpu.get_barrier_semaphore()
     after = lax.rem(me + 1, 128)
     before = lax.rem(me + 127, 128)
@@ -125,6 +127,8 @@
     flags[:, :SLOTS] = jnp.broadcast_to(
         jnp.where(mask_ref[...] == 1, 1.0, 0.0), (16, SLOTS)
     )
+    featured[0] = jnp.zeros((128, 512), jnp.bfloat16)
+    featured[0, :SLOTS, 384:] = jnp.ones((SLOTS, 128), jnp.bfloat16)
     any_token[...] = jnp.full_like(any_token, -1)
     any_token[:, :SLOTS] = jnp.broadcast_to(token_ref[...], (8, SLOTS))
     own_flags = flags[...].astype(jnp.bfloat16)
@@ -133,21 +137,12 @@
     halo_out[1, :SIDE] = atoms_ref[:SIDE]
     halo_out[0, SIDE:] = own_flags
     halo_out[1, SIDE:] = own_flags
-    live_token[...] = jnp.where(flags[:8] > 0.5, any_token[...], -1)
+    live_token[0] = jnp.where(flags[:8] > 0.5, any_token[...], -1)
     pl.semaphore_wait(barrier, 24)
     copy(halo_out.at[0], halo_in.at[0], 6, after // 8, lax.rem(after, 8))
     copy(halo_out.at[1], halo_in.at[1], 7, before // 8, lax.rem(before, 8))
     for step in range(1, 16):
         greet(entered, lax.rem(r + step, 16), c)
-
-    for k in range(7, 11):
-        loads[k].wait()
-    for w in range(6):
-        weights[pl.ds(w * 128, 128), :] = _flip(out_w_ref[w])
-        weights[pl.ds((6 + w) * 128, 128), :] = _flip(in_w_ref[w])
-    for w in range(2):
-        tin_t[pl.ds(w * 512, 512), :] = _flip(tin_ref[w])
-    tout_t[...] = _flip(tout_ref[...])
 
     own = atoms_ref[...].astype(jnp.float32)
     own_normed = _norm_rows(own).astype(jnp.bfloat16)
@@ -200,51 +195,88 @@
     atom_mid = resid + _dot(hidden, atom_tout_ref[...])
     mid[...] = atom_mid
     feature = jnp.maximum(_dot(atom_mid.astype(jnp.bfloat16), token_in_ref[...]), 0.0)
-    featured[...] = jnp.zeros_like(featured)
-    featured[:SLOTS, :384] = feature.astype(jnp.bfloat16)
-    featured[:SLOTS, 384:] = jnp.ones((SLOTS, 128), jnp.bfloat16)
-
+    featured[0, :SLOTS, :384] = feature.astype(jnp.bfloat16)
+    copy(featured.at[0], featured.at[1], 8, sibling, c)
+    copy(live_token.at[0], live_token.at[1], 9, sibling, c)
+
+    await_bytes(featured.at[0], sent.at[8])
+    await_bytes(live_token.at[0], sent.at[9])
+    await_bytes(featured.at[1], got.at[8])
+    await_bytes(live_token.at[1], got.at[9])
+    slots_token = jnp.concatenate([live_token[0, :1], live_token[1, :1]], 1)
+    both = featured[...].reshape(256, 512)
+    place = lax.broadcasted_iota(jnp.int32, (64, 256), 0)
+    owner = place // 8 * 16 + core * 8 + place % 8
     for t in range(4):
-        owner = lax.broadcasted_iota(jnp.int32, (128, 128), 0)
-        member = _ones_where(owner * 4 + t == live_token[:1])
-        sums = _dot(member, featured[...])
+        sums = _dot(_ones_where(owner * 4 + t == slots_token), both)
         for m in range(4):
-            rows32[pl.ds(4 * m + t, 128, stride=16), :] = sums[:, m * 128 : (m + 1) * 128]
-
-    def pack(target):
-        def move(d, _):
-            target[pl.ds(d * 8, 8)] = (
-                rows32[pl.ds(d * 128, 128), :].reshape(8, 16, 128).astype(jnp.bfloat16)
-            )
-            return 0
-
-        lax.fori_loop(0, 16, move, 0)
-
-    def launch(source, target, k):
-        target[me] = source[me]
-        for row, col in peers:
-            copy(source.at[row * 8 + col], target.at[me], k, row, col)
+            rows32[pl.ds(4 * m + t, 64, stride=16), :] = sums[:, m * 128 : (m + 1) * 128]
+
+    def pack(target, first, count):
+        target[first : first + count] = (
+            rows32[first * 16 : (first + count) * 16].reshape(count, 16, 128).astype(jnp.bfloat16)
+        )
+
+    def launch(source, target, k, slot):
+        target[slot] = source[me]
+        for row, col, _, _ in chips:
+            copy(source.at[row * 8 + col], target.at[slot], k, row, col)
+            copy(source.at[row * 8 + 8 + col], target.at[slot], k, row + 1, col)
+        copy(source.at[sibling * 8 + c], target.at[slot], k, sibling, c)
+
+    def launch_quarter(source, target, k, half, turn):
+        first = half * 64 + lax.rem(parity + turn, 2) * 32
+        for row, col, place, shift_parity in chips:
+            if shift_parity == turn:
+                copy(source.at[first + place], target.at[me], k, row + half, col)
 
     def finish_copies(source, target, k):
         part = pl.ds(0, 127)
         await_bytes(source.at[part], sent.at[k])
         await_bytes(target.at[part], got.at[k])
 
-    pack(send_t)
+    pack(send_t, 0, 64)
     pl.semaphore_wait(entered, 15)
-    launch(send_t, recv_t, 8)
-    finish_copies(send_t, recv_t, 8)
-
-    def gather_sums(d, total):
-        return total + jnp.sum(recv_t[pl.ds(d * 8, 8)].astype(jnp.float32), 0)
-
-    total = lax.fori_loop(0, 16, gather_sums, jnp.zeros((16, 128), jnp.float32))
+    chip_place = (r // 2) * 8 + c
+    recv_t[chip_place] = send_t[chip_place]
+    for row, col, _, _ in chips:
+        copy(send_t.at[row * 4 + col], recv_t.at[chip_place], 12, row + core, col)
+
+    for k in range(7, 11):
+        loads[k].wait()
+    for t, source in enumerate((out_w_ref, in_w_ref)):
+        for w in range(4):
+            turned = _flip(source[w])
+            for quarter in range(4):
+                place = t * 768 + quarter * 128 + w * 32
+                weights[place : place + 32] = turned[quarter * 32 : quarter * 32 + 32]
+        for w in (4, 5):
+            weights[t * 768 + w * 128 : t * 768 + w * 128 + 128] = _flip(source[w])
+    for w in range(2):
+        tin_t[w * 512 : w * 512 + 512] = _flip(tin_ref[w])
+    tout_t[...] = _flip(tout_ref[...])
+    loads[0].wait()
+    for a in range(16):
+        natural = jnp.concatenate([pair_ref[a], pair_ref[a + 16]], 0).astype(jnp.float32)
+        state[:, a * 128 : a * 128 + 128] = jnp.transpose(natural)
+        row = lax.broadcasted_iota(jnp.int32, (128, 128), 0)
+        lane = lax.broadcasted_iota(jnp.int32, (128, 128), 1)
+        right_token = jnp.where(row % 8 >= 4, row // 8 * 4 + row % 8 - 4, -1)
+        spreader[:128, a * 128 : a * 128 + 128] = _ones_where(lane % 64 == right_token)
+        left_token = jnp.where(row % 16 < 4, row // 16 * 4 + row % 16, -1)
+        spreader[128:, a * 128 : a * 128 + 128] = _ones_where(
+            jnp.where(lane < 64, a, a + 16) == left_token
+        )
     loads[6].wait()
+    await_bytes(send_t.at[pl.ds(0, 63)], sent.at[12])
+    await_bytes(recv_t.at[pl.ds(0, 63)], got.at[12])
+
+    total = jnp.zeros((16, 128), jnp.float32)
+    for d in range(0, 64, 32):
+        total = total + jnp.sum(recv_t[d : d + 32].astype(jnp.float32), 0)
     count = jnp.maximum(total[12:], 1.0)
-    proj = jnp.zeros((4, 384), jnp.float32)
-    for m in range(3):
-        single = (total[4 * m : 4 * m + 4] / count).astype(jnp.bfloat16)
-        proj = proj + _dot(single, token_out_ref[pl.ds(m * 128, 128), :])
+    single = jnp.concatenate([total[4 * m : 4 * m + 4] / count for m in range(3)], 1)
+    proj = _dot(single.astype(jnp.bfloat16), token_out_ref[...])
     share[...] = jnp.zeros_like(share)
     for m in range(3):
         share[4 * m : 4 * m + 4] = proj[:, m * 128 : (m + 1) * 128]
@@ -252,8 +284,6 @@
     recv_row[c] = share[...]
     column = me // 16
     place = lax.rem(me, 16)
-    for step in range(1, 8):
-        copy(share, recv_row.at[c], 9, r, lax.rem(c + step, 8))
     for step in range(1, 16):
         row = lax.rem(r + step, 16)
         copy(share.at[pl.ds(0, 8)], recv_right.at[place], 10, row, column)
@@ -265,9 +295,16 @@
     @pl.when(column != c)
     def _():
         copy(share.at[pl.ds(0, 8)], recv_right.at[place], 10, r, column)
+
+    for step in range(1, 8):
+        copy(share, recv_row.at[c], 13, r, lax.rem(c + step, 8))
+
+    @pl.when(column != c)
+    def _():
         await_bytes(recv_right.at[pl.ds(0, 1)], sent.at[10])
+
     await_bytes(recv_right.at[pl.ds(0, 15)], sent.at[10])
-    await_bytes(recv_row.at[pl.ds(0, 7)], sent.at[9])
+    await_bytes(recv_row.at[pl.ds(0, 7)], sent.at[13])
 
     mine = (me >= 16 * c) & (me < 16 * c + 16)
 
@@ -279,18 +316,7 @@
     def _():
         await_bytes(recv_right, got.at[10])
 
-    await_bytes(recv_row.at[pl.ds(0, 7)], got.at[9])
-    for j in range(16):
-        right64[4 * j : 4 * j + 4] = recv_right[j, 4:8]
-    for j in range(8):
-        left32[4 * j : 4 * j + 4] = recv_row[j, :4]
-        add32[4 * j : 4 * j + 4] = recv_row[j, 8:12]
-    recv_add[r] = add32[...]
-    for step in range(1, 16):
-        copy(add32, recv_add.at[r], 11, lax.rem(r + step, 16), c)
-
-    loads[0].wait()
-
+    await_bytes(recv_row.at[pl.ds(0, 7)], got.at[13])
     def spans(width, step):
         if width == 2048:
             step(0)
@@ -300,30 +326,45 @@
     def lanes(g, width):
         return pl.ds(g * width if isinstance(g, int) else pl.multiple_of(g * width, width), width)
 
+    over_rows = (((0,), (0,)), ((), ()))
+    rows = jnp.concatenate(
+        [recv_right[...].reshape(128, 128), recv_row[...].reshape(128, 128)], 0
+    )
+    high = rows.astype(jnp.bfloat16)
+    low = (rows - high.astype(jnp.float32)).astype(jnp.bfloat16)
+
     def start_state(g):
-        right = right64[...]
-        for h in range(START // 128):
-            a = g * (START // 128) + h
-            natural = jnp.concatenate([pair_ref[a], pair_ref[a + 16]], 0).astype(jnp.float32)
-            natural = natural + jnp.concatenate(
-                [right + left32[pl.ds(a, 1), :], right + left32[pl.ds(a + 16, 1), :]], 0
-            )
-            turned = jnp.transpose(natural)
-            state[:, lanes(a, 128)] = turned
-            normed[:, lanes(a, 128)] = _norm(turned).astype(jnp.bfloat16)
+        here = lanes(g, START)
+        spread = spreader[:, here]
+        started = (
+            state[:, here]
+            + lax.dot_general(high, spread, over_rows, preferred_element_type=jnp.float32)
+            + lax.dot_general(low, spread, over_rows, preferred_element_type=jnp.float32)
+        )
+        state[:, here] = started
+        normed[:, here] = _norm(started).astype(jnp.bfloat16)
 
     spans(START, start_state)
 
-    def edges(base, first):
+    def edges(t, half, turn, target):
+        quarter = half * 2 + lax.rem(parity + turn, 2)
+        stage = (half * 2 + turn) * 1024
+        place = pl.ds(pl.multiple_of(t * 768 + quarter * 128, 128), 128)
+
         def chunk(g):
-            both = _dot(weights[pl.ds((base + first) * 128, 256), :], normed[:, lanes(g, EDGE)])
-            edge = _sigmoid(both[:128]) * both[128:]
+            both = _dot(weights[place, :], normed[:, lanes(g, EDGE)])
+            left = _sigmoid(both[:32]) * both[32:64]
+            right = _sigmoid(both[64:96]) * both[96:]
             for h in range(EDGE // 128):
-                rows32[pl.ds(g * (EDGE // 128) + h, 128, stride=16), :] = edge[
-                    :, h * 128 : (h + 1) * 128
-                ]
+                a = stage + g * (EDGE // 128) + h
+                part = slice(h * 128, h * 128 + 128)
+                edge32[pl.ds(a, 32, stride=32), :] = left[:, part]
+                edge32[pl.ds(a + 16, 32, stride=32), :] = right[:, part]
 
         spans(EDGE, chunk)
+        target[pl.ds(quarter * 32, 32)] = (
+            edge32[stage : stage + 1024].reshape(32, 32, 128).astype(jnp.bfloat16)
+        )
 
     def gates(base):
         def chunk(g):
@@ -335,13 +376,13 @@
 
     low_lanes = lax.broadcasted_iota(jnp.int32, (16, 128), 1) < 64
 
-    def assemble(source, target):
+    def assemble(source, first, target):
         def block(g, _):
             for k in range(ROWS):
                 row = g * ROWS + k
                 for q in range(4):
-                    even = source[row * 8 + 2 * q]
-                    odd = source[row * 8 + 2 * q + 1]
+                    even = source[row * 8 + 2 * q, first : first + 16]
+                    odd = source[row * 8 + 2 * q + 1, first : first + 16]
                     target[pl.ds(row * 32, 16), pl.ds(q * 128, 128)] = jnp.where(
                         low_lanes, even, pltpu.roll(odd, 64, 1)
                     )
@@ -365,19 +406,18 @@
 
         lax.fori_loop(0, 16 // ROWS, block, 0)
 
-    def triangle(t, width, after):
+    def triangle(t, width, beside, after):
         base = 6 * t
-        edges(base, 0)
-        pack(send_l.at[t])
-        launch(send_l.at[t], recv_l.at[t], 3 * t)
-        edges(base, 2)
-        pack(send_r.at[t])
-        launch(send_r.at[t], recv_r.at[t], 3 * t + 1)
+        for half in range(2):
+            for turn in range(2):
+                edges(t, half, turn, send_e.at[t])
+                launch_quarter(send_e.at[t], recv_e.at[t], 2 * t, half, turn)
+        copy(send_e.at[t, sibling_channel], recv_e.at[t, me], 2 * t, sibling, c)
+        recv_e[t, me] = send_e[t, channel]
         gates(base)
-        finish_copies(send_l.at[t], recv_l.at[t], 3 * t)
-        assemble(recv_l.at[t], mat_l)
-        finish_copies(send_r.at[t], recv_r.at[t], 3 * t + 1)
-        assemble(recv_r.at[t], mat_r)
+        finish_copies(send_e.at[t], recv_e.at[t], 2 * t)
+        assemble(recv_e.at[t], 0, mat_l)
+        assemble(recv_e.at[t], 16, mat_r)
         axis = 1 - t
         mat_p[...] = lax.dot_general(
             mat_l[...],
@@ -386,16 +426,14 @@
             preferred_element_type=jnp.float32,
         ).astype(jnp.bfloat16)
         split(mat_p, send_p.at[t])
-        launch(send_p.at[t], recv_p.at[t], 3 * t + 2)
-        finish_copies(send_p.at[t], recv_p.at[t], 3 * t + 2)
-
-        def widen(d, _):
-            rows32[pl.ds(d * 128, 128), :] = (
-                recv_p[t, pl.ds(d * 8, 8)].astype(jnp.float32).reshape(128, 128)
-            )
-            return 0
-
-        lax.fori_loop(0, 16, widen, 0)
+        launch(send_p.at[t], recv_p.at[t], 2 * t + 1, channel)
+        beside()
+        finish_copies(send_p.at[t], recv_p.at[t], 2 * t + 1)
+
+        if t == 0:
+            for step in range(1, 16):
+                copy(add32, recv_add.at[r], 11, lax.rem(r + step, 16), c)
+        rows32[...] = recv_p[t].astype(jnp.float32).reshape(2048, 128)
 
         def close(g):
             count = width // 128
@@ -425,28 +463,32 @@
             result_ref[g * (width // 128) + h] = natural[:64]
             result_ref[g * (width // 128) + h + 16] = natural[64:]
 
-    triangle(0, CLOSE, next_update)
-    triangle(1, LAST, transition)
-
-    await_bytes(recv_add.at[pl.ds(0, 15)], sent.at[11])
-    await_bytes(recv_add.at[pl.ds(0, 15)], got.at[11])
-    added = recv_add[...].reshape(512, 128)
-    high = added.astype(jnp.bfloat16)
-    low = (added - high.astype(jnp.float32)).astype(jnp.bfloat16)
-    token = lax.broadcasted_iota(jnp.int32, (512, 128), 0)
-    chosen = _ones_where(token == any_token[:1])
-    over = (((0,), (0,)), ((), ()))
-    picked = lax.dot_general(
-        chosen, high, over, preferred_element_type=jnp.float32
-    ) + lax.dot_general(chosen, low, over, preferred_element_type=jnp.float32)
-    atoms_out_ref[...] = (mid[...] + picked[:SLOTS]).astype(jnp.bfloat16)
+    def share_added():
+        for j in range(8):
+            add32[4 * j : 4 * j + 4] = recv_row[j, 8:12]
+        recv_add[r] = add32[...]
+
+    def finish_atoms():
+        await_bytes(recv_add.at[pl.ds(0, 15)], sent.at[11])
+        await_bytes(recv_add.at[pl.ds(0, 15)], got.at[11])
+        added = recv_add[...].reshape(512, 128)
+        high = added.astype(jnp.bfloat16)
+        low = (added - high.astype(jnp.float32)).astype(jnp.bfloat16)
+        token = lax.broadcasted_iota(jnp.int32, (512, 128), 0)
+        chosen = _ones_where(token == any_token[:1])
+        picked = lax.dot_general(
+            chosen, high, over_rows, preferred_element_type=jnp.float32
+        ) + lax.dot_general(chosen, low, over_rows, preferred_element_type=jnp.float32)
+        atoms_out_ref[...] = (mid[...] + picked[:SLOTS]).astype(jnp.bfloat16)
+
+    triangle(0, CLOSE, share_added, next_update)
+    triangle(1, LAST, finish_atoms, transition)
 
 
 def body(pair_in, atoms_in, atom_token, atom_mask, *parameters):
     vmem = pl.BlockSpec(memory_space=pltpu.VMEM)
     staged = (pair_in, atoms_in, *parameters)
     bf16, f32 = jnp.bfloat16, jnp.float32
-    message = (2, 128, 16, 128)
     return pl.pallas_call(
         _kernel,
         out_shape=(
@@ -465,28 +507,29 @@
             pltpu.VMEM((1024, 128), bf16),
             pltpu.VMEM((128, 512), bf16),
         ]
-        + [pltpu.VMEM(message, bf16)] * 6
+        + [pltpu.VMEM((2, 128, 32, 128), bf16)] * 2
+        + [pltpu.VMEM((4096, 128), f32)]
+        + [pltpu.VMEM((2, 128, 16, 128), bf16)] * 2
         + [pltpu.VMEM((512, 512), bf16)] * 3
         + [
             pltpu.VMEM((2, 64, 128), bf16),
             pltpu.VMEM((2, 64, 128), bf16),
             pltpu.VMEM((16, 128), f32),
-            pltpu.VMEM((8, 128), jnp.int32),
+            pltpu.VMEM((2, 8, 128), jnp.int32),
             pltpu.VMEM((8, 128), jnp.int32),
             pltpu.VMEM((WIDE, 128), bf16),
             pltpu.VMEM((SLOTS, 128), f32),
-            pltpu.VMEM((128, 512), bf16),
-            pltpu.VMEM((128, 16, 128), bf16),
-            pltpu.VMEM((128, 16, 128), bf16),
+            pltpu.VMEM((2, 128, 512), bf16),
+            pltpu.VMEM((64, 16, 128), bf16),
+            pltpu.VMEM((64, 16, 128), bf16),
             pltpu.VMEM((16, 128), f32),
             pltpu.VMEM((8, 16, 128), f32),
             pltpu.VMEM((16, 8, 128), f32),
-            pltpu.VMEM((32, 128), f32),
-            pltpu.VMEM((64, 128), f32),
+            pltpu.VMEM((256, 2048), bf16),
             pltpu.VMEM((32, 128), f32),
             pltpu.VMEM((16, 32, 128), f32),
-            pltpu.SemaphoreType.DMA((12,)),
-            pltpu.SemaphoreType.DMA((12,)),
+            pltpu.SemaphoreType.DMA((14,)),
+            pltpu.SemaphoreType.DMA((14,)),
             pltpu.SemaphoreType.REGULAR,
             pltpu.SemaphoreType.DMA((11,)),
         ],

time: 93.1 us -> 88.5 us (0.951)
  Pallas kernels: 89.8 us -> 85.2 us
    pallas_call x1, Pallas kernels: 89.8 us -> 85.2 us  [body(): pl.pallas_call(_kernel, out_shape=(jax.ShapeDtypeStruct(pair_in.shape, bf...]
where the time goes in v4:
time: 88.5 us; the launch traced here: 88.3 us
  Pallas kernels  85.2 us (96%)
  local copies, waits for them, and re-layouts  2.49 us (3%)
    pallas_call x1, Pallas kernels, body(): pl.pallas_call(_kernel, out_shape=(jax.ShapeDtypeStruct(pair_in.shape, bf...  85.2 us
    unnamed x4, local copies, waits for them, and re-layouts  2.49 us

profile of v4, /device:TPU:1, one launch (start us, length us, event | category | flops | bytes accessed | tf_op | source)
XLA Modules:
  0.0 88.3 jit_solution(9328111631986635492)
XLA Ops:
  0.6 85.2 %atoms_and_pair.1 = (bf16[32,64,128]{2,1,0:T(8,128)(2,1)}, bf16[96,128]{1,0:T(8,128)(2,1)}) custom-call(s32[1,96]{1,0:T(1,128)} %bitcast.2, s32[1,96]{1,0:T(1,128)} %bitcast.3, bf16[32,64,128]{2,1,0:T(8,128)(2,1)} %refs_0_.1, bf16[96,128]{1,0:T(8,128)(2,1)} %refs_1_.1, bf16[5,128,128]{2,1,0:T(8,128)(2,1)} %refs_2_.1, bf16[2,128,256]{2,1,0:T(8,128)(2,1)} %refs_3_.1, ...), custom_call_target="tpu_custom_call" | custom-call | tf_op jit(solution)/shard_map/atoms_and_pair/pallas_call | solution.py:492
  85.8 0.0 copy-start
  85.8 1.9 %copy.17 = bf16[32,64,128]{2,1,0:T(8,128)(2,1)} copy(bf16[32,64,128]{2,1,0:T(8,128)(2,1)} %get-tuple-element.4) | data formatting | bytes 1048576
  87.7 0.0 copy-done
  87.7 0.6 copy.18
Async XLA Ops:
  85.8 1.9 %copy-start = (bf16[96,128]{1,0:T(8,128)(2,1)S(1)}, bf16[96,128]{1,0:T(8,128)(2,1)}, u32[]{:S(2)}) copy-start(bf16[96,128]{1,0:T(8,128)(2,1)} %get-tuple-element.5) | copy-start | bytes 73732

commit v5 on v4

--- a/solution.py
+++ b/solution.py
@@ -219,9 +219,9 @@
 
     def launch(source, target, k, slot):
         target[slot] = source[me]
-        for row, col, _, _ in chips:
-            copy(source.at[row * 8 + col], target.at[slot], k, row, col)
-            copy(source.at[row * 8 + 8 + col], target.at[slot], k, row + 1, col)
+        for half in range(2):
+            for row, col, _, _ in chips:
+                copy(source.at[row * 8 + half * 8 + col], target.at[slot], k, row + half, col)
         copy(source.at[sibling * 8 + c], target.at[slot], k, sibling, c)
 
     def launch_quarter(source, target, k, half, turn):
@@ -489,7 +489,7 @@
     vmem = pl.BlockSpec(memory_space=pltpu.VMEM)
     staged = (pair_in, atoms_in, *parameters)
     bf16, f32 = jnp.bfloat16, jnp.float32
-    return pl.pallas_call(
+    pair_out, atoms_out = pl.pallas_call(
         _kernel,
         out_shape=(
             jax.ShapeDtypeStruct(pair_in.shape, bf16),
@@ -539,6 +539,38 @@
         name="atoms_and_pair",
     )(atom_token.reshape(1, SLOTS), atom_mask.reshape(1, SLOTS), *staged)
 
+    def hand_over(pair_ref, atoms_ref, pair_to, atoms_to, pair_held, atoms_held, loaded, stored):
+        parts = [(pair_ref.at[pl.ds(k * 8, 8)], pair_held.at[pl.ds(k * 8, 8)], pair_to.at[pl.ds(k * 8, 8)])
+                 for k in range(4)] + [(atoms_ref, atoms_held, atoms_to)]
+        loads = [pltpu.make_async_copy(a, b, loaded.at[k]) for k, (a, b, _) in enumerate(parts)]
+        stores = [pltpu.make_async_copy(b, c, stored.at[k]) for k, (_, b, c) in enumerate(parts)]
+        for load in loads:
+            load.start()
+        for load, store in zip(loads, stores):
+            load.wait()
+            store.start()
+        for store in stores:
+            store.wait()
+
+    hbm = pl.BlockSpec(memory_space=pl.ANY)
+    return pl.pallas_call(
+        hand_over,
+        out_shape=(
+            jax.ShapeDtypeStruct(pair_in.shape, bf16),
+            jax.ShapeDtypeStruct(atoms_in.shape, bf16),
+        ),
+        in_specs=[hbm] * 2,
+        out_specs=(hbm, hbm),
+        scratch_shapes=[
+            pltpu.VMEM(pair_in.shape, bf16),
+            pltpu.VMEM(atoms_in.shape, bf16),
+            pltpu.SemaphoreType.DMA((5,)),
+            pltpu.SemaphoreType.DMA((5,)),
+        ],
+        compiler_params=pltpu.CompilerParams(vmem_limit_bytes=60 * 1024 * 1024),
+        name="hand_over",
+    )(pair_out, atoms_out)
+
 
 def solution(mesh):
     placed = (

time: 88.5 us -> 87.7 us (level)
  local copies, waits for them, and re-layouts: 2.49 us -> 0 us
  Pallas kernels: 85.2 us -> 86.7 us
    unnamed x4 -> x0, local copies, waits for them, and re-layouts: 2.49 us -> none
    pallas_call x0 -> x1, Pallas kernels: none -> 1.84 us  [body(): pl.pallas_call(hand_over, out_shape=(jax.ShapeDtypeStruct(pair_in.shape,...]
where the time goes in v5:
time: 87.7 us; the launch traced here: 87.5 us
  Pallas kernels  86.7 us (99%)
    pallas_call x1, Pallas kernels, body(): pl.pallas_call(_kernel, out_shape=(jax.ShapeDtypeStruct(pair_in.shape, bf...  84.9 us
    pallas_call x1, Pallas kernels, body(): pl.pallas_call(hand_over, out_shape=(jax.ShapeDtypeStruct(pair_in.shape,...  1.84 us

profile of v5, /device:TPU:1, one launch (start us, length us, event | category | flops | bytes accessed | tf_op | source)
XLA Modules:
  0.0 87.5 jit_solution(8431429702526343001)
XLA Ops:
  0.6 84.9 %atoms_and_pair.1 = (bf16[32,64,128]{2,1,0:T(8,128)(2,1)}, bf16[96,128]{1,0:T(8,128)(2,1)}) custom-call(s32[1,96]{1,0:T(1,128)} %bitcast.2, s32[1,96]{1,0:T(1,128)} %bitcast.3, bf16[32,64,128]{2,1,0:T(8,128)(2,1)} %refs_0_.1, bf16[96,128]{1,0:T(8,128)(2,1)} %refs_1_.1, bf16[5,128,128]{2,1,0:T(8,128)(2,1)} %refs_2_.1, bf16[2,128,256]{2,1,0:T(8,128)(2,1)} %refs_3_.1, ...), custom_call_target="tpu_custom_call" | custom-call | tf_op jit(solution)/shard_map/atoms_and_pair/pallas_call | solution.py:492
  85.5 1.8 %hand_over.1 = (bf16[32,64,128]{2,1,0:T(8,128)(2,1)}, bf16[96,128]{1,0:T(8,128)(2,1)}) custom-call(bf16[32,64,128]{2,1,0:T(8,128)(2,1)} %get-tuple-element.4.pair_ref, bf16[96,128]{1,0:T(8,128)(2,1)} %get-tuple-element.5.atoms_ref), custom_call_target="tpu_custom_call" | custom-call | tf_op jit(solution)/shard_map/hand_over/pallas_call | solution.py:556

commit v6 on v5

--- a/solution.py
+++ b/solution.py
@@ -77,7 +77,7 @@
     (    state, normed, gate, rows32, weights, tin_t, tout_t,
     send_e, recv_e, edge32, send_p, recv_p, mat_l, mat_r, mat_p,
     halo_out, halo_in, flags, live_token, any_token, wide, mid, featured,
-    send_t, recv_t, share, recv_row, recv_right, spreader, add32, recv_add,
+    send_t, recv_t, share, recv_row, recv_right, spreader, add32, added_rows, recv_add,
     sent, got, entered, loaded) = refs
     r = lax.axis_index("row")
     c = lax.axis_index("col")
@@ -416,6 +416,9 @@
         recv_e[t, me] = send_e[t, channel]
         gates(base)
         finish_copies(send_e.at[t], recv_e.at[t], 2 * t)
+        if t == 1:
+            for step in range(1, 16):
+                copy(added_rows, recv_add.at[r], 11, lax.rem(r + step, 16), c)
         assemble(recv_e.at[t], 0, mat_l)
         assemble(recv_e.at[t], 16, mat_r)
         axis = 1 - t
@@ -430,9 +433,6 @@
         beside()
         finish_copies(send_p.at[t], recv_p.at[t], 2 * t + 1)
 
-        if t == 0:
-            for step in range(1, 16):
-                copy(add32, recv_add.at[r], 11, lax.rem(r + step, 16), c)
         rows32[...] = recv_p[t].astype(jnp.float32).reshape(2048, 128)
 
         def close(g):
@@ -466,19 +466,20 @@
     def share_added():
         for j in range(8):
             add32[4 * j : 4 * j + 4] = recv_row[j, 8:12]
-        recv_add[r] = add32[...]
+        added_rows[...] = add32[...].astype(jnp.bfloat16)
+        recv_add[r] = added_rows[...]
 
     def finish_atoms():
         await_bytes(recv_add.at[pl.ds(0, 15)], sent.at[11])
         await_bytes(recv_add.at[pl.ds(0, 15)], got.at[11])
-        added = recv_add[...].reshape(512, 128)
-        high = added.astype(jnp.bfloat16)
-        low = (added - high.astype(jnp.float32)).astype(jnp.bfloat16)
         token = lax.broadcasted_iota(jnp.int32, (512, 128), 0)
         chosen = _ones_where(token == any_token[:1])
         picked = lax.dot_general(
-            chosen, high, over_rows, preferred_element_type=jnp.float32
-        ) + lax.dot_general(chosen, low, over_rows, preferred_element_type=jnp.float32)
+            chosen,
+            recv_add[...].reshape(512, 128),
+            over_rows,
+            preferred_element_type=jnp.float32,
+        )
         atoms_out_ref[...] = (mid[...] + picked[:SLOTS]).astype(jnp.bfloat16)
 
     triangle(0, CLOSE, share_added, next_update)
@@ -527,7 +528,8 @@
             pltpu.VMEM((16, 8, 128), f32),
             pltpu.VMEM((256, 2048), bf16),
             pltpu.VMEM((32, 128), f32),
-            pltpu.VMEM((16, 32, 128), f32),
+            pltpu.VMEM((32, 128), bf16),
+            pltpu.VMEM((16, 32, 128), bf16),
             pltpu.SemaphoreType.DMA((14,)),
             pltpu.SemaphoreType.DMA((14,)),
             pltpu.SemaphoreType.REGULAR,

time: 87.7 us -> 85.5 us (0.975)
  Pallas kernels: 86.7 us -> 84.5 us
    pallas_call x1, Pallas kernels: 84.9 us -> 82.7 us  [body(): pl.pallas_call(_kernel, out_shape=(jax.ShapeDtypeStruct(pair_in.shape, bf...]
where the time goes in v6:
time: 85.5 us; the launch traced here: 85.3 us
  Pallas kernels  84.5 us (99%)
    pallas_call x1, Pallas kernels, body(): pl.pallas_call(_kernel, out_shape=(jax.ShapeDtypeStruct(pair_in.shape, bf...  82.7 us
    pallas_call x1, Pallas kernels, body(): pl.pallas_call(hand_over, out_shape=(jax.ShapeDtypeStruct(pair_in.shape,...  1.84 us

profile of v6, /device:TPU:1, one launch (start us, length us, event | category | flops | bytes accessed | tf_op | source)
XLA Modules:
  0.0 85.3 jit_solution(14647543226902951311)
XLA Ops:
  0.6 82.7 %atoms_and_pair.1 = (bf16[32,64,128]{2,1,0:T(8,128)(2,1)}, bf16[96,128]{1,0:T(8,128)(2,1)}) custom-call(s32[1,96]{1,0:T(1,128)} %bitcast.2, s32[1,96]{1,0:T(1,128)} %bitcast.3, bf16[32,64,128]{2,1,0:T(8,128)(2,1)} %refs_0_.1, bf16[96,128]{1,0:T(8,128)(2,1)} %refs_1_.1, bf16[5,128,128]{2,1,0:T(8,128)(2,1)} %refs_2_.1, bf16[2,128,256]{2,1,0:T(8,128)(2,1)} %refs_3_.1, ...), custom_call_target="tpu_custom_call" | custom-call | tf_op jit(solution)/shard_map/atoms_and_pair/pallas_call | solution.py:493
  83.3 1.8 %hand_over.1 = (bf16[32,64,128]{2,1,0:T(8,128)(2,1)}, bf16[96,128]{1,0:T(8,128)(2,1)}) custom-call(bf16[32,64,128]{2,1,0:T(8,128)(2,1)} %get-tuple-element.4.pair_ref, bf16[96,128]{1,0:T(8,128)(2,1)} %get-tuple-element.5.atoms_ref), custom_call_target="tpu_custom_call" | custom-call | tf_op jit(solution)/shard_map/hand_over/pallas_call | solution.py:558

commit v7 on v6

--- a/solution.py
+++ b/solution.py
@@ -409,7 +409,7 @@
     def triangle(t, width, beside, after):
         base = 6 * t
         for half in range(2):
-            for turn in range(2):
+            for turn in (1, 0):
                 edges(t, half, turn, send_e.at[t])
                 launch_quarter(send_e.at[t], recv_e.at[t], 2 * t, half, turn)
         copy(send_e.at[t, sibling_channel], recv_e.at[t, me], 2 * t, sibling, c)

time: 85.5 us -> 85.3 us (level)
  no operation moved by 1% of the time
where the time goes in v7:
time: 85.3 us; the launch traced here: 85.2 us
  Pallas kernels  84.4 us (99%)
    pallas_call x1, Pallas kernels, body(): pl.pallas_call(_kernel, out_shape=(jax.ShapeDtypeStruct(pair_in.shape, bf...  82.5 us
    pallas_call x1, Pallas kernels, body(): pl.pallas_call(hand_over, out_shape=(jax.ShapeDtypeStruct(pair_in.shape,...  1.84 us

profile of v7, /device:TPU:1, one launch (start us, length us, event | category | flops | bytes accessed | tf_op | source)
XLA Modules:
  0.0 85.2 jit_solution(17111488332355292746)
XLA Ops:
  0.6 82.5 %atoms_and_pair.1 = (bf16[32,64,128]{2,1,0:T(8,128)(2,1)}, bf16[96,128]{1,0:T(8,128)(2,1)}) custom-call(s32[1,96]{1,0:T(1,128)} %bitcast.2, s32[1,96]{1,0:T(1,128)} %bitcast.3, bf16[32,64,128]{2,1,0:T(8,128)(2,1)} %refs_0_.1, bf16[96,128]{1,0:T(8,128)(2,1)} %refs_1_.1, bf16[5,128,128]{2,1,0:T(8,128)(2,1)} %refs_2_.1, bf16[2,128,256]{2,1,0:T(8,128)(2,1)} %refs_3_.1, ...), custom_call_target="tpu_custom_call" | custom-call | tf_op jit(solution)/shard_map/atoms_and_pair/pallas_call | solution.py:493
  83.2 1.8 %hand_over.1 = (bf16[32,64,128]{2,1,0:T(8,128)(2,1)}, bf16[96,128]{1,0:T(8,128)(2,1)}) custom-call(bf16[32,64,128]{2,1,0:T(8,128)(2,1)} %get-tuple-element.4.pair_ref, bf16[96,128]{1,0:T(8,128)(2,1)} %get-tuple-element.5.atoms_ref), custom_call_target="tpu_custom_call" | custom-call | tf_op jit(solution)/shard_map/hand_over/pallas_call | solution.py:558
